TPU v7x, 256 devices: a whole 4x4x8 slice. The times are simulated.
256 devices in a mesh: dp: 8 (over x, core), point: 32 (over z, y).
Axes of the slice: x: 4, y: 4, z: 8, core: 2. Of those that a mesh axis runs over, the one named last changes fastest.
Arguments:
- material_points: bfloat16 [8, 16384, 256], P('dp', 'point'), may hold values from -16 to 16
- loss_sensitivity: bfloat16 [8, 16384, 256], P('dp', 'point'), may hold values from -6 to 6
- averaged_quantity_linear: bfloat16 [256, 256], replicated, may hold values from -0.375 to 0.375
- partition_choosing_linear: bfloat16 [256, 256], replicated, may hold values from -0.375 to 0.375
- partition_assigning_linear: bfloat16 [32, 64], replicated, may hold values from -2 to 2
- summary_point_linears: bfloat16 [32, 96], replicated, may hold values from -2 to 2
- closing_linear_map: bfloat16 [256, 256], replicated, may hold values from -0.375 to 0.375
- expanding_linear_map: bfloat16 [256, 1024], replicated, may hold values from -0.375 to 0.375
- contracting_linear_map: bfloat16 [1024, 256], replicated, may hold values from -0.1875 to 0.1875
- softmax_sharpness: float32 [8], replicated, may hold values from 0.5 to 2
Outputs:
- updated: bfloat16 [8, 16384, 256], P('dp', 'point')
- particle_grad: bfloat16 [8, 16384, 256], P('dp', 'point')
- feature_grad: float32 [256, 256], replicated
- project_grad: float32 [256, 256], replicated
- slice_grad: float32 [32, 64], replicated
- token_grad: float32 [32, 96], replicated
- output_grad: float32 [256, 256], replicated
- up_grad: float32 [256, 1024], replicated
- down_grad: float32 [1024, 256], replicated
All inputs are finite; a program needn't handle non-finite values.
Results may differ from a plain program's by a relative error of at most 0.03.
Values sent between devices are 32-bit elements; how exact they have to be, the bound alone decides.
A program may use at most 64 MiB of HBM per device.

v0:
```python
import jax
import jax.numpy as jnp
from jax import lax
from jax.sharding import PartitionSpec as P

eps_norm = 1e-05
eps_mass = 1e-05
gelu_coef = 0.7978845608028654


def normalize(values):
    values = values.astype(jnp.float32)
    center = values - jnp.mean(values, axis=-1, keepdims=True)
    inverse = lax.rsqrt(jnp.mean(center * center, axis=-1, keepdims=True) + eps_norm)
    return (center * inverse, inverse)


def normalize_back(normed, inverse, incoming):
    mean_grad = jnp.mean(incoming, axis=-1, keepdims=True)
    mean_proj = jnp.mean(incoming * normed, axis=-1, keepdims=True)
    return inverse * (incoming - mean_grad - normed * mean_proj)


def gelu_pair(hidden):
    inner = gelu_coef * (hidden + 0.044715 * hidden * hidden * hidden)
    tangent = jnp.tanh(inner)
    activated = 0.5 * hidden * (1.0 + tangent)
    gelu_slope = 0.5 * (1.0 + tangent) + 0.5 * hidden * (1.0 - tangent * tangent) * gelu_coef * (
        1.0 + 3.0 * 0.044715 * hidden * hidden
    )
    return (activated, gelu_slope)


def token_mix(slice_feature_totals, slice_mass, token_single_float):
    per_head_width = slice_feature_totals.shape[2]
    slice_tokens = slice_feature_totals / (slice_mass + eps_mass)[:, :, None]
    projection_rows = jnp.einsum(
        "wzg,gl->wzl", slice_tokens, token_single_float, precision=lax.Precision.HIGHEST
    )
    slice_query_rows = projection_rows[:, :, :per_head_width]
    slice_key_rows = projection_rows[:, :, per_head_width : 2 * per_head_width]
    slice_value_rows = projection_rows[:, :, 2 * per_head_width :]
    attention_scores = jnp.einsum(
        "vts,vzs->vtz", slice_query_rows, slice_key_rows, precision=lax.Precision.HIGHEST
    ) * per_head_width ** (-0.5)
    exponent = jnp.exp(attention_scores)
    attention_result = exponent / jnp.sum(exponent, axis=-1, keepdims=True)
    return jnp.einsum(
        "yew,ywa->yea", attention_result, slice_value_rows, precision=lax.Precision.HIGHEST
    )


def body(
    material_points,
    loss_sensitivity,
    averaged_quantity_linear,
    partition_choosing_linear,
    partition_assigning_linear,
    summary_point_linears,
    closing_linear_map,
    expanding_linear_map,
    contracting_linear_map,
    softmax_sharpness,
):
    thirty_two_bit_kind = jnp.float32
    bfloat_sixteen_kind = jnp.bfloat16
    particle_row_count = material_points.shape[1]
    hidden_model_width = material_points.shape[2]
    per_head_width = partition_assigning_linear.shape[0]
    head_count = hidden_model_width // per_head_width
    entering_material_entries = material_points[0]
    sensitivity_entering_entries = loss_sensitivity[0]
    normed, inverse = normalize(entering_material_entries)
    normed_half = normed.astype(bfloat_sixteen_kind)
    features = jnp.dot(
        normed_half, averaged_quantity_linear, preferred_element_type=thirty_two_bit_kind
    ).astype(bfloat_sixteen_kind)
    projection_rows = jnp.dot(
        normed_half, partition_choosing_linear, preferred_element_type=thirty_two_bit_kind
    ).astype(bfloat_sixteen_kind)
    feature_per_head = features.reshape(particle_row_count, head_count, per_head_width)
    linear_image_each_group = projection_rows.reshape(
        particle_row_count, head_count, per_head_width
    )
    partition_energy_entries = (
        jnp.einsum(
            "gnj,jv->gnv",
            linear_image_each_group,
            partition_assigning_linear,
            preferred_element_type=thirty_two_bit_kind,
        )
        / softmax_sharpness[None, :, None]
    )
    exponent = jnp.exp(partition_energy_entries)
    partition_membership_share = exponent / jnp.sum(exponent, axis=-1, keepdims=True)
    slice_probability_low = partition_membership_share.astype(bfloat_sixteen_kind)
    totals_piece = jnp.einsum(
        "cts,ctl->tsl",
        slice_probability_low,
        feature_per_head,
        preferred_element_type=thirty_two_bit_kind,
    )
    mass_part = jnp.sum(partition_membership_share, axis=0)
    slice_feature_totals, slice_mass = lax.psum((totals_piece, mass_part), "point")
    mixed, pullback = jax.vjp(
        token_mix,
        slice_feature_totals,
        slice_mass,
        summary_point_linears.astype(thirty_two_bit_kind),
    )
    token_blend_low = mixed.astype(bfloat_sixteen_kind)
    broadcast_rows = (
        jnp.einsum(
            "wov,ovc->woc",
            slice_probability_low,
            token_blend_low,
            preferred_element_type=thirty_two_bit_kind,
        )
        .astype(bfloat_sixteen_kind)
        .reshape(particle_row_count, hidden_model_width)
    )
    residual = (
        entering_material_entries.astype(thirty_two_bit_kind)
        + jnp.dot(broadcast_rows, closing_linear_map, preferred_element_type=thirty_two_bit_kind)
    ).astype(bfloat_sixteen_kind)
    normed2, inverse2 = normalize(residual)
    normed2_half = normed2.astype(bfloat_sixteen_kind)
    hidden = jnp.dot(normed2_half, expanding_linear_map, preferred_element_type=thirty_two_bit_kind)
    activated, gelu_slope = gelu_pair(hidden)
    activated_half = activated.astype(bfloat_sixteen_kind)
    updated = (
        residual.astype(thirty_two_bit_kind)
        + jnp.dot(
            activated_half, contracting_linear_map, preferred_element_type=thirty_two_bit_kind
        )
    ).astype(bfloat_sixteen_kind)
    grad_hidden = (
        jnp.dot(
            sensitivity_entering_entries,
            contracting_linear_map.T,
            preferred_element_type=thirty_two_bit_kind,
        )
        * gelu_slope
    ).astype(bfloat_sixteen_kind)
    grad_normed2 = jnp.dot(
        grad_hidden, expanding_linear_map.T, preferred_element_type=thirty_two_bit_kind
    )
    grad_residual = sensitivity_entering_entries.astype(thirty_two_bit_kind) + normalize_back(
        normed2, inverse2, grad_normed2
    )
    grad_residual_half = grad_residual.astype(bfloat_sixteen_kind)
    grad_spread = jnp.dot(
        grad_residual_half, closing_linear_map.T, preferred_element_type=thirty_two_bit_kind
    ).astype(bfloat_sixteen_kind)
    broadcast_per_head = grad_spread.reshape(particle_row_count, head_count, per_head_width)
    token_blend_piece = jnp.einsum(
        "cts,ctl->tsl",
        slice_probability_low,
        broadcast_per_head,
        preferred_element_type=thirty_two_bit_kind,
    )
    gradient_token_blend = lax.psum(token_blend_piece, "point")
    grad_sums, gradient_slice_weight_total, grad_tokenmap = pullback(gradient_token_blend)
    gradient_totals_low = grad_sums.astype(bfloat_sixteen_kind)
    sensitivity_assignment_share = jnp.einsum(
        "wgv,gzv->wgz",
        broadcast_per_head,
        token_blend_low,
        preferred_element_type=thirty_two_bit_kind,
    )
    sensitivity_assignment_share = (
        sensitivity_assignment_share
        + jnp.einsum(
            "wgv,gzv->wgz",
            feature_per_head,
            gradient_totals_low,
            preferred_element_type=thirty_two_bit_kind,
        )
        + gradient_slice_weight_total[None]
    )
    gradient_feature_rows = (
        jnp.einsum(
            "wov,ovc->woc",
            slice_probability_low,
            gradient_totals_low,
            preferred_element_type=thirty_two_bit_kind,
        )
        .astype(bfloat_sixteen_kind)
        .reshape(particle_row_count, hidden_model_width)
    )
    sensitivity_partition_energies = (
        partition_membership_share
        * (
            sensitivity_assignment_share
            - jnp.sum(
                partition_membership_share * sensitivity_assignment_share, axis=-1, keepdims=True
            )
        )
        / softmax_sharpness[None, :, None]
    ).astype(bfloat_sixteen_kind)
    grad_projected = (
        jnp.einsum(
            "rhm,dm->rhd",
            sensitivity_partition_energies,
            partition_assigning_linear,
            preferred_element_type=thirty_two_bit_kind,
        )
        .astype(bfloat_sixteen_kind)
        .reshape(particle_row_count, hidden_model_width)
    )
    grad_normed = jnp.dot(
        gradient_feature_rows,
        averaged_quantity_linear.T,
        preferred_element_type=thirty_two_bit_kind,
    ) + jnp.dot(
        grad_projected, partition_choosing_linear.T, preferred_element_type=thirty_two_bit_kind
    )
    particle_grad = (grad_residual + normalize_back(normed, inverse, grad_normed)).astype(
        bfloat_sixteen_kind
    )
    grad_scale = (lax.axis_size("dp") * lax.axis_size("point") * particle_row_count) ** (-0.5)
    feature_term = (
        jnp.einsum(
            "rc,rf->cf",
            normed_half,
            gradient_feature_rows,
            preferred_element_type=thirty_two_bit_kind,
        )
        * grad_scale
    )
    project_term = (
        jnp.einsum(
            "rc,rf->cf", normed_half, grad_projected, preferred_element_type=thirty_two_bit_kind
        )
        * grad_scale
    )
    slice_term = (
        jnp.einsum(
            "rhd,rhm->dm",
            linear_image_each_group,
            sensitivity_partition_energies,
            preferred_element_type=thirty_two_bit_kind,
        )
        * grad_scale
    )
    output_term = (
        jnp.einsum(
            "rc,rf->cf",
            broadcast_rows,
            grad_residual_half,
            preferred_element_type=thirty_two_bit_kind,
        )
        * grad_scale
    )
    up_term = (
        jnp.einsum(
            "rc,rf->cf", normed2_half, grad_hidden, preferred_element_type=thirty_two_bit_kind
        )
        * grad_scale
    )
    down_term = (
        jnp.einsum(
            "rf,rc->fc",
            activated_half,
            sensitivity_entering_entries,
            preferred_element_type=thirty_two_bit_kind,
        )
        * grad_scale
    )
    token_term = grad_tokenmap * (grad_scale / lax.axis_size("point"))
    totals = lax.psum(
        (feature_term, project_term, slice_term, token_term, output_term, up_term, down_term),
        ("dp", "point"),
    )
    return (
        updated[None],
        particle_grad[None],
        totals[0],
        totals[1],
        totals[2],
        totals[3],
        totals[4],
        totals[5],
        totals[6],
    )


def solution(mesh):
    in_specs = (
        P("dp", "point", None),
        P("dp", "point", None),
        P(),
        P(),
        P(),
        P(),
        P(),
        P(),
        P(),
        P(),
    )
    out_specs = (P("dp", "point", None), P("dp", "point", None), P(), P(), P(), P(), P(), P(), P())
    return jax.shard_map(body, mesh=mesh, in_specs=in_specs, out_specs=out_specs, check_vma=False)
```

profile of v0, /device:TPU:1, one launch (start us, length us, event | category | flops | bytes accessed | tf_op | source)
XLA Modules:
  0.0 602.0 jit_solution(4008141565221524528)
XLA Ops:
  7.3 1.1 copy.19
  8.6 1.2 convolution_convert_fusion.4
  9.8 1.3 convolution_convert_fusion.5
  11.1 1.4 fusion.80
  12.6 0.9 fusion.85
  13.6 64.6 %psum.71 = f32[8,64]{1,0:T(8,128)S(1)} all-reduce(f32[8,64]{1,0:T(8,128)S(1)} %get-tuple-element.29), channel_id=1, replica_groups=mesh['dp'=8,'point'=32] {'point'}, use_global_device_ids=true, to_apply=%region_5.0 | all-reduce | flops 512 | bytes 4096 | tf_op jit(solution)/shard_map/psum | solution.py:104
  78.4 76.1 %all-reduce.9.cloned.1.call-done = f32[8,64,32]{1,2,0:T(8,128)} async-done(((f32[8,64,32]{1,2,0:T(8,128)}), f32[8,64,32]{1,2,0:T(8,128)}) %all-reduce.9.cloned.1.call-update) | async-done | bytes 65552 | tf_op jit(solution)/shard_map/psum | solution.py:104
  154.5 1.3 fusion.69
  155.8 0.6 fusion.81
  156.5 0.7 convolution_convert_fusion.6
  157.4 0.3 fusion.82
  157.8 0.5 fusion.67
  158.3 0.4 copy-done.22
  158.7 1.6 fusion.19
  160.3 1.4 fusion.7
  161.8 1.9 convolution_multiply_fusion
  163.7 0.5 fusion.79
  164.3 1.4 convolution_multiply_fusion.1
  165.9 1.0 convolution_multiply_fusion.2
  166.8 0.2 convolution_convert_fusion.1
  167.1 0.9 fusion.86
  168.0 0.3 fusion.87
  168.4 0.2 all-reduce.13.cloned.1.call-start
  168.6 0.6 multiply_divide_fusion.1
  169.2 1.8 copy.34
  171.0 136.6 %all-reduce.11.cloned.1.call-done = f32[8,64,32]{1,2,0:T(8,128)} async-done(((f32[8,64,32]{1,2,0:T(8,128)}), f32[8,64,32]{1,2,0:T(8,128)}) %all-reduce.11.cloned.1.call-update) | async-done | bytes 65552 | tf_op jit(solution)/shard_map/psum | solution.py:162
  307.6 1.5 multiply_reduce_fusion.3
  309.1 1.6 fusion.53
  310.8 1.6 fusion.56
  312.4 0.5 fusion.65
  313.0 0.3 multiply_reduce_fusion.4
  313.3 0.3 copy-done.15
  313.8 1.0 convolution_multiply_fusion.4
  314.8 0.2 fusion.88
  315.1 1.3 fusion.12
  316.4 2.6 convolution_convert_fusion
  319.0 1.0 convolution_multiply_fusion.3
  320.1 0.3 fusion.78
  320.5 0.8 copy.35
  321.4 0.4 fusion.21
  321.8 2.6 fusion.20
  324.4 78.5 %all-reduce.3 = (f32[32,64]{1,0:T(8,128)}, f32[32,96]{1,0:T(8,128)}) all-reduce(f32[32,64]{1,0:T(8,128)S(1)} %fusion.20, f32[32,96]{1,0:T(8,128)S(1)} %fusion.21), channel_id=1, replica_groups=mesh['dp'=8,'point'=32] {'dp','point'}, use_global_device_ids=true, to_apply=%region_19.0 | all-reduce | flops 5120 | bytes 40960 | tf_op jit(solution)/shard_map/psum | solution.py:271
  402.9 184.2 %all-reduce.13.cloned.1.call-done = (f32[256,256]{1,0:T(8,128)}, f32[256,256]{1,0:T(8,128)}, f32[256,256]{1,0:T(8,128)}, f32[256,1024]{1,0:T(8,128)}, f32[1024,256]{1,0:T(8,128)}) async-done(((f32[256,256]{1,0:T(8,128)}, f32[256,256]{1,0:T(8,128)}, f32[256,256]{1,0:T(8,128)}, f32[256,1024]{1,0:T(8,128)}, f32[1024,256]{1,0:T(8,128)}), (f32[256,256]{1,0:T(8,128)}, f32[256,256]{1,0:T(8,128)}, ...) | async-done | bytes 2883600 | tf_op jit(solution)/shard_map/psum | solution.py:271
  587.1 1.8 copy.56
  588.9 1.7 copy.57
  590.5 1.7 copy.58
  592.2 2.3 copy.59
  594.5 1.0 copy.60
  (79 shorter events, 1.5 us)
Async XLA Ops:
  7.2 150.6 %copy-start = (bf16[256,1024]{1,0:T(8,128)(2,1)S(1)}, bf16[256,1024]{1,0:T(8,128)(2,1)}, u32[]{:S(2)}) copy-start(bf16[256,1024]{1,0:T(8,128)(2,1)} %param.17) | copy-start | bytes 1572868
  7.2 3.9 copy-start.25
  7.2 3.9 copy-start.23
  7.2 147.3 %all-reduce.9.cloned.1.call-start = ((), (), s32[]{:S(2)}) async-start(), calls=%async_computation | async-start | bytes 262144 | tf_op jit(solution)/shard_map/psum | solution.py:104
  9.8 2.8 copy-start.1
  11.1 1.5 copy-start.27
  11.1 67.1 %copy-start.7 = (bf16[1,512,256]{2,1,0:T(8,128)(2,1)S(1)}, bf16[1,512,256]{2,1,0:T(8,128)(2,1)}, u32[]{:S(2)}) copy-start(bf16[1,512,256]{2,1,0:T(8,128)(2,1)} %param.11) | copy-start | bytes 786436
  11.1 143.4 %copy-start.20 = (bf16[32,96]{1,0:T(8,128)(2,1)S(1)}, bf16[32,96]{1,0:T(8,128)(2,1)}, u32[]{:S(2)}) copy-start(bf16[32,96]{1,0:T(8,128)(2,1)} %param.15) | copy-start | bytes 18436
  13.5 143.9 %copy-start.6 = (bf16[256,256]{1,0:T(8,128)(2,1)S(1)}, bf16[256,256]{1,0:T(8,128)(2,1)}, u32[]{:S(2)}) copy-start(bf16[256,256]{1,0:T(8,128)(2,1)} %param.16) | copy-start | bytes 393220
  13.5 294.1 %all-reduce.11.cloned.1.call-start = ((), (), s32[]{:S(2)}) async-start(), calls=%async_computation.1 | async-start | bytes 262144 | tf_op jit(solution)/shard_map/psum | solution.py:162
  156.4 1.8 copy-start.3
  156.4 12.2 %copy-start.18 = (f32[8,64]{1,0:T(8,128)}, f32[8,64]{1,0:T(8,128)S(1)}, u32[]{:S(2)}) copy-start(f32[8,64]{1,0:T(8,128)S(1)} %get-tuple-element.34) | copy-start | bytes 6148
  157.7 1.0 copy-start.22
  168.3 144.0 %copy-start.4 = (f32[8,64,64]{1,2,0:T(8,128)S(1)}, f32[8,64,64]{1,2,0:T(8,128)}, u32[]{:S(2)}) copy-start(f32[8,64,64]{1,2,0:T(8,128)} %copy-done.3) | copy-start | bytes 393220
  168.4 418.7 %all-reduce.13.cloned.1.call-start = ((), (), s32[]{:S(2)}) async-start(), calls=%async_computation.2 | async-start | bytes 5767168 | tf_op jit(solution)/shard_map/psum | solution.py:271
  171.0 141.9 %copy-start.10 = (f32[8,64,32]{1,2,0:T(8,128)S(1)}, f32[8,64,32]{1,2,0:T(8,128)}, u32[]{:S(2)}) copy-start(f32[8,64,32]{1,2,0:T(8,128)} %all-reduce.9.cloned.1.call-done) | copy-start | bytes 196612
  307.6 3.1 copy-start.19
  307.6 4.8 copy-start.9
  307.6 5.4 copy-start.21
  310.7 4.1 copy-start.11
  310.7 4.1 copy-start.8
  312.4 2.7 copy-start.13
  312.4 2.7 copy-start.2
  312.9 0.7 copy-start.15
  313.8 2.6 copy-start.24
  313.8 2.6 copy-start.26
  319.0 1.0 copy-start.17
  320.0 1.3 copy-start.12
  320.0 1.3 copy-start.14
  320.0 1.3 copy-start.16
  320.1 1.8 copy-start.28
  587.1 7.4 %copy-start.5 = (f32[1024,256]{1,0:T(8,128)S(1)}, f32[1024,256]{1,0:T(8,128)}, u32[]{:S(2)}) copy-start(f32[1024,256]{1,0:T(8,128)} %get-tuple-element.54) | copy-start | bytes 3145732
Sparse Core Ops, SparseCore 0:
  13.6 140.7 all-reduce.8
  168.5 139.0 all-reduce.10
  320.1 266.9 all-reduce.12
where the time goes:
time: 603 us; the launch traced here: 602 us
  waiting for transfers between devices  397 us (66%)
  blocking collectives  143 us (24%)
  matrix products  33 us (5%)
  between operations  14.3 us (2%)
  local copies, waits for them, and re-layouts  13.2 us (2%)
    psum x1, waiting for transfers between devices, body(): lax.psum((feature_term, project_term, slice_term, token_term, output_term...  184 us
    psum x1, waiting for transfers between devices, body(): gradient_token_blend = lax.psum(token_blend_piece, 'point')  137 us
    psum x1, blocking collectives, body(): lax.psum((feature_term, project_term, slice_term, token_term, output_term...  78.5 us
    psum x1, waiting for transfers between devices, body(): lax.psum((totals_piece, mass_part), 'point')  76.1 us
    psum x1, blocking collectives, body(): lax.psum((totals_piece, mass_part), 'point')  64.6 us
    unnamed x67, local copies, waits for them, and re-layouts  13.2 us
  transfers between devices with their start and end apart: 3, of which 3 were waited for; matrix products, arithmetic and copies ran while one was open for 1% of the time, Pallas kernels for 0%

commit v1 on v0

v1 whole, which is shorter than its diff:
```python
import functools

import jax
import jax.numpy as jnp
from jax import lax
from jax.experimental import pallas as pl
from jax.experimental.pallas import tpu as pltpu
from jax.sharding import PartitionSpec as P

F32 = jnp.float32
BF16 = jnp.bfloat16
MESH = pl.DeviceIdType.MESH
EPS = 1e-05
GELU = 0.7978845608028654
HIGH = lax.Precision.HIGHEST

NX, NC, NZ, NY = 4, 2, 8, 4
ROWS = 512
C, FF, HEADS, HD, SL = 256, 1024, 8, 32, 64
PAIRS = 4
KXY = NX * NY
EROWS = 72
LROWS = 17
CH = 128


def dot(a, b):
    return jnp.dot(a, b, preferred_element_type=F32)


def dot_t(a, b):
    return lax.dot_general(a, b, (((1,), (1,)), ((), ())), preferred_element_type=F32)


def tdot(a, b):
    return lax.dot_general(a, b, (((0,), (0,)), ((), ())), preferred_element_type=F32)


def hdot(a, b, dims):
    return lax.dot_general(
        a, b, ((dims[:1], dims[1:]), ((), ())), precision=HIGH, preferred_element_type=F32
    )


def norm_rows(v):
    center = v - jnp.mean(v, axis=-1, keepdims=True)
    inv = lax.rsqrt(jnp.mean(center * center, axis=-1, keepdims=True) + EPS)
    return center * inv, inv


def norm_back(normed, inv, g):
    return inv * (
        g - jnp.mean(g, axis=-1, keepdims=True) - normed * jnp.mean(g * normed, axis=-1, keepdims=True)
    )


def seg_sum(v, ones):
    hi = v.astype(BF16)
    lo = (v - hi.astype(F32)).astype(BF16)
    return jnp.concatenate(
        [
            dot(hi[:, 256 * g : 256 * g + 256], ones) + dot(lo[:, 256 * g : 256 * g + 256], ones)
            for g in range(2)
        ],
        axis=1,
    )


def each(n, f):
    def step(i, carry):
        f(i)
        return carry

    lax.fori_loop(0, n, step, 0)


def remote(src, dst, ss, rs, dev):
    return pltpu.make_async_remote_copy(
        src_ref=src, dst_ref=dst, send_sem=ss, recv_sem=rs, device_id=dev, device_id_type=MESH
    )


SCRATCH = dict(
    mp=pltpu.VMEM((ROWS, C), BF16),
    ls=pltpu.VMEM((ROWS, C), BF16),
    wa=pltpu.VMEM((C, C), BF16),
    wp=pltpu.VMEM((C, C), BF16),
    ws=pltpu.VMEM((HD, SL), BF16),
    wt=pltpu.VMEM((HD, 3 * HD), BF16),
    wc=pltpu.VMEM((C, C), BF16),
    we=pltpu.VMEM((C, FF), BF16),
    wd=pltpu.VMEM((FF, C), BF16),
    in_sem=pltpu.SemaphoreType.DMA((9,)),
    nh=pltpu.VMEM((ROWS, C), BF16),
    feat=pltpu.VMEM((ROWS, C), BF16),
    proj=pltpu.VMEM((ROWS, C), BF16),
    asg=pltpu.VMEM((ROWS, 512), F32),
    ah=pltpu.VMEM((ROWS, 512), BF16),
    bdw=pltpu.VMEM((C, 512), BF16),
    bdm=pltpu.VMEM((C, 512), BF16),
    bdg=pltpu.VMEM((C, 512), BF16),
    ones=pltpu.VMEM((256, 256), BF16),
    spread=pltpu.VMEM((ROWS, C), BF16),
    n2h=pltpu.VMEM((ROWS, C), BF16),
    act=pltpu.VMEM((ROWS, FF), BF16),
    gh=pltpu.VMEM((ROWS, FF), BF16),
    gres=pltpu.VMEM((ROWS, C), F32),
    grh=pltpu.VMEM((ROWS, C), BF16),
    gspr=pltpu.VMEM((ROWS, C), BF16),
    ga=pltpu.VMEM((ROWS, 512), F32),
    gl=pltpu.VMEM((ROWS, 512), BF16),
    gf=pltpu.VMEM((ROWS, C), BF16),
    gp=pltpu.VMEM((ROWS, C), BF16),
    upd=pltpu.VMEM((ROWS, C), BF16),
    pgr=pltpu.VMEM((ROWS, C), BF16),
    a_p=pltpu.VMEM((PAIRS, 40, 128), F32),
    a_y=pltpu.VMEM((3, 40, 128), F32),
    a_z=pltpu.VMEM((NZ, 40, 128), F32),
    a_m=pltpu.VMEM((PAIRS, HD, 128), F32),
    a_ys=pltpu.SemaphoreType.DMA((2, 3)),
    a_zs=pltpu.SemaphoreType.DMA((2, 7)),
    a_ms=pltpu.SemaphoreType.DMA((2, 3)),
    b_p=pltpu.VMEM((PAIRS, HD, 128), F32),
    b_y=pltpu.VMEM((3, HD, 128), F32),
    b_z=pltpu.VMEM((NZ, HD, 128), F32),
    b_m=pltpu.VMEM((PAIRS, 40, 128), F32),
    b_ys=pltpu.SemaphoreType.DMA((2, 3)),
    b_zs=pltpu.SemaphoreType.DMA((2, 7)),
    b_ms=pltpu.SemaphoreType.DMA((2, 3)),
    e_all=pltpu.VMEM((2 * KXY, EROWS, C), F32),
    e_core=pltpu.VMEM((KXY, EROWS, C), F32),
    e_xy=pltpu.VMEM((KXY - 1, EROWS, C), F32),
    e_part=pltpu.VMEM((EROWS, C), F32),
    e_z=pltpu.VMEM((NZ, 8, C), F32),
    e_zo=pltpu.VMEM((NZ, 8, C), F32),
    e_fin=pltpu.VMEM((2 * KXY, EROWS, C), F32),
    e_cs=pltpu.SemaphoreType.DMA((2,)),
    e_xys=pltpu.SemaphoreType.DMA((2, KXY - 1)),
    e_zs=pltpu.SemaphoreType.DMA((2, 7)),
    e_zos=pltpu.SemaphoreType.DMA((2, 7)),
    e_zgs=pltpu.SemaphoreType.DMA((2, 7)),
    e_xygs=pltpu.SemaphoreType.DMA((2, KXY - 1)),
    e_cgs=pltpu.SemaphoreType.DMA((2,)),
    l_all=pltpu.VMEM((2 * KXY, LROWS, C), F32),
    l_core=pltpu.VMEM((KXY, LROWS, C), F32),
    l_xy=pltpu.VMEM((KXY - 1, LROWS, C), F32),
    l_z=pltpu.VMEM((NZ, LROWS, C), F32),
    l_fin=pltpu.VMEM((2 * KXY, LROWS, C), F32),
    l_cs=pltpu.SemaphoreType.DMA((2,)),
    l_xys=pltpu.SemaphoreType.DMA((2, KXY - 1)),
    l_zs=pltpu.SemaphoreType.DMA((2, 7)),
    l_xygs=pltpu.SemaphoreType.DMA((2, KXY - 1)),
    l_cgs=pltpu.SemaphoreType.DMA((2,)),
    out_sem=pltpu.SemaphoreType.DMA((10,)),
)


class Names:
    pass


def kernel(scale, *refs):
    ins, rest = refs[:10], refs[10:]
    (o_upd, o_pg, o_feat, o_proj, o_slice, o_tok, o_out, o_up, o_down) = rest[:9]
    s = Names()
    for name, ref in zip(SCRATCH, rest[9:]):
        setattr(s, name, ref)

    dp, pt = lax.axis_index("dp"), lax.axis_index("point")
    x, c = dp // NC, dp % NC
    z, y = pt // NY, pt % NY
    k = x * NY + y
    own = c * KXY + k
    other = (x * NC + (1 - c), pt)

    def at_y(i):
        return lax.rem(y + i + 1, NY)

    def from_y(i):
        return lax.rem(y + NY - 1 - i, NY)

    def at_z(i):
        return lax.rem(z + i + 1, NZ)

    def from_z(i):
        return lax.rem(z + NZ - 1 - i, NZ)

    def at_xy(i):
        j = i + 1
        return lax.rem(x + j // NY, NX), lax.rem(y + j % NY, NY)

    def from_xy(i):
        j = i + 1
        return lax.rem(x + NX - j // NY, NX), lax.rem(y + NY - j % NY, NY)

    def dev_y(yy):
        return (dp, z * NY + yy)

    def dev_z(zz):
        return (dp, zz * NY + y)

    def dev_xy(xx, yy):
        return (xx * NC + c, z * NY + yy)

    barrier = pltpu.get_barrier_semaphore()
    pl.semaphore_signal(barrier, inc=1, device_id=other, device_id_type=MESH)
    each(
        KXY - 1,
        lambda i: pl.semaphore_signal(
            barrier, inc=1, device_id=dev_xy(*at_xy(i)), device_id_type=MESH
        ),
    )
    each(
        NZ - 1,
        lambda i: pl.semaphore_signal(barrier, inc=1, device_id=dev_z(at_z(i)), device_id_type=MESH),
    )

    in_dst = (s.mp, s.ls, s.wa, s.wp, s.ws, s.wt, s.wc, s.we, s.wd)
    loads = [pltpu.make_async_copy(a, b, s.in_sem.at[i]) for i, (a, b) in enumerate(zip(ins, in_dst))]
    order = (0, 2, 3, 4, 5, 1, 6, 7, 8)
    for i in order:
        loads[i].start()
    sharp_ref = ins[9]

    lane = lax.broadcasted_iota(jnp.int32, (1, 512), 1)
    sharp = jnp.full((1, 512), sharp_ref[0], F32)
    for h in range(1, HEADS):
        sharp = jnp.where(lane // SL == h, sharp_ref[h], sharp)
    inv_sharp = 1.0 / sharp
    rr = lax.broadcasted_iota(jnp.int32, (256, 256), 0)
    cc = lax.broadcasted_iota(jnp.int32, (256, 256), 1)
    s.ones[...] = jnp.where(rr // SL == cc // SL, 1.0, 0.0).astype(BF16)
    s.bdm[...] = jnp.zeros_like(s.bdm)
    s.bdg[...] = jnp.zeros_like(s.bdg)
    low = lax.broadcasted_iota(jnp.int32, (HD, 128), 1) < SL

    def pack_diag(t):
        return jnp.where(low, t[:HD], t[HD:])

    def spread_diag(v):
        return jnp.concatenate([jnp.where(low, v, 0.0), jnp.where(low, 0.0, v)], axis=0).astype(BF16)

    loads[4].wait()
    w1 = s.ws[...].astype(F32)
    w2 = jnp.concatenate([w1, w1], axis=1)
    s.bdw[...] = jnp.zeros_like(s.bdw)
    for j in range(PAIRS):
        s.bdw[64 * j : 64 * j + 64, 128 * j : 128 * j + 128] = spread_diag(w2)

    for i in (0, 2, 3):
        loads[i].wait()
    mass = jnp.zeros((1, 512), F32)
    for r in range(0, ROWS, CH):
        rows = slice(r, r + CH)
        normed, _ = norm_rows(s.mp[rows, :].astype(F32))
        nh = normed.astype(BF16)
        s.nh[rows, :] = nh
        s.feat[rows, :] = dot(nh, s.wa[...]).astype(BF16)
        proj = dot(nh, s.wp[...]).astype(BF16)
        s.proj[rows, :] = proj
        logits = (
            jnp.concatenate(
                [
                    dot(
                        proj[:, 128 * g : 128 * g + 128],
                        s.bdw[128 * g : 128 * g + 128, 256 * g : 256 * g + 256],
                    )
                    for g in range(2)
                ],
                axis=1,
            )
            * inv_sharp
        )
        e = jnp.exp(logits)
        a = e / seg_sum(e, s.ones[...])
        s.asg[rows, :] = a
        s.ah[rows, :] = a.astype(BF16)
        mass = mass + jnp.sum(a, axis=0, keepdims=True)

    def head_sums(values, out):
        for g in range(2):
            t = tdot(values[:, 128 * g : 128 * g + 128], s.ah[:, 256 * g : 256 * g + 256])
            for j in range(2):
                out[2 * g + j, 0:HD, :] = pack_diag(
                    t[64 * j : 64 * j + 64, 128 * j : 128 * j + 128]
                )

    head_sums(s.feat, s.a_p)
    for j in range(PAIRS):
        s.a_p[j, HD:, :] = jnp.broadcast_to(mass[:, 128 * j : 128 * j + 128], (8, 128))

    def reduce_pairs(part, buf_y, buf_z, sem_y, sem_z):
        def put_y(i):
            t = at_y(i)
            return remote(part.at[t], buf_y.at[i], sem_y.at[0, i], sem_y.at[1, i], dev_y(t))

        def put_z(i):
            return remote(
                buf_z.at[z], buf_z.at[z], sem_z.at[0, i], sem_z.at[1, i], dev_z(at_z(i))
            )

        def got_z(i):
            f = from_z(i)
            return remote(buf_z.at[f], buf_z.at[f], sem_z.at[0, i], sem_z.at[1, i], dev_z(f))

        def start():
            each(NY - 1, lambda i: put_y(i).start())

        def middle():
            each(NY - 1, lambda i: put_y(i).wait_recv())
            buf_z[z] = part[y] + buf_y[0] + buf_y[1] + buf_y[2]
            each(NZ - 1, lambda i: put_z(i).start())

        def finish():
            each(NZ - 1, lambda i: got_z(i).wait_recv())
            total = buf_z[0]
            for i in range(1, NZ):
                total = total + buf_z[i]
            return total

        def drain():
            each(NY - 1, lambda i: put_y(i).wait_send())
            each(NZ - 1, lambda i: put_z(i).wait_send())

        return start, middle, finish, drain

    def gather_pairs(buf, sem):
        def put(i):
            return remote(buf.at[y], buf.at[y], sem.at[0, i], sem.at[1, i], dev_y(at_y(i)))

        def got(i):
            f = from_y(i)
            return remote(buf.at[f], buf.at[f], sem.at[0, i], sem.at[1, i], dev_y(f))

        def start():
            each(NY - 1, lambda i: put(i).start())

        def wait():
            each(NY - 1, lambda i: got(i).wait_recv())

        def drain():
            each(NY - 1, lambda i: put(i).wait_send())

        return start, wait, drain

    pl.semaphore_wait(barrier, 1 + (KXY - 1) + (NZ - 1))
    a_start, a_middle, a_finish, a_drain = reduce_pairs(s.a_p, s.a_y, s.a_z, s.a_ys, s.a_zs)
    am_start, am_wait, am_drain = gather_pairs(s.a_m, s.a_ms)
    a_start()
    a_middle()
    for i in (5, 1, 6, 7, 8):
        loads[i].wait()
    total = a_finish()

    wt = s.wt[...].astype(F32)
    inv_mass = 1.0 / (total[HD : HD + 1] + EPS)
    tokens = total[:HD] * inv_mass
    qkv = hdot(wt, tokens, (0, 0))
    q, kk, v = qkv[:HD], qkv[HD : 2 * HD], qkv[2 * HD :]
    r2 = lax.broadcasted_iota(jnp.int32, (128, 128), 0) // SL
    c2 = lax.broadcasted_iota(jnp.int32, (128, 128), 1) // SL
    scores = hdot(q, kk, (0, 0)) * HD ** (-0.5)
    expo = jnp.where(r2 == c2, jnp.exp(jnp.where(r2 == c2, scores, 0.0)), 0.0)
    att = expo / jnp.sum(expo, axis=-1, keepdims=True)
    s.a_m[y] = hdot(v, att, (1, 1))
    am_start()
    am_wait()
    for j in range(PAIRS):
        s.bdm[64 * j : 64 * j + 64, 128 * j : 128 * j + 128] = spread_diag(s.a_m[j])

    for r in range(0, ROWS, CH):
        rows = slice(r, r + CH)
        spread = jnp.concatenate(
            [
                dot_t(
                    s.ah[rows, 256 * g : 256 * g + 256],
                    s.bdm[128 * g : 128 * g + 128, 256 * g : 256 * g + 256],
                )
                for g in range(2)
            ],
            axis=1,
        ).astype(BF16)
        s.spread[rows, :] = spread
        res = (s.mp[rows, :].astype(F32) + dot(spread, s.wc[...])).astype(BF16).astype(F32)
        n2, inv2 = norm_rows(res)
        n2h = n2.astype(BF16)
        s.n2h[rows, :] = n2h
        sens = s.ls[rows, :]
        upd = res
        gn2 = jnp.zeros((CH, C), F32)
        for f in range(0, FF, 256):
            hid = dot(n2h, s.we[:, f : f + 256])
            gact = dot_t(sens, s.wd[f : f + 256, :])
            h2 = hid * hid
            u = 0.5 + 0.5 * jnp.tanh(hid * (GELU + GELU * 0.044715 * h2))
            act = hid * u
            slope = u + act * (1.0 - u) * (2.0 * GELU + 6.0 * GELU * 0.044715 * h2)
            acth = act.astype(BF16)
            gh = (gact * slope).astype(BF16)
            s.act[rows, f : f + 256] = acth
            s.gh[rows, f : f + 256] = gh
            upd = upd + dot(acth, s.wd[f : f + 256, :])
            gn2 = gn2 + dot_t(gh, s.we[:, f : f + 256])
        s.upd[rows, :] = upd.astype(BF16)
        gres = sens.astype(F32) + norm_back(n2, inv2, gn2)
        s.gres[rows, :] = gres
        grh = gres.astype(BF16)
        s.grh[rows, :] = grh
        s.gspr[rows, :] = dot_t(grh, s.wc[...]).astype(BF16)

    head_sums(s.gspr, s.b_p)
    b_start, b_middle, b_finish, b_drain = reduce_pairs(s.b_p, s.b_y, s.b_z, s.b_ys, s.b_zs)
    bm_start, bm_wait, bm_drain = gather_pairs(s.b_m, s.b_ms)
    b_start()
    out_upd = pltpu.make_async_copy(s.upd, o_upd, s.out_sem.at[0])
    out_upd.start()

    for b in range(4):
        s.e_all[:, 8 * b : 8 * b + 8, :] = tdot(
            s.n2h[...], s.gh[:, 256 * b : 256 * b + 256]
        ).reshape(32, 8, C)
    for b in range(4):
        s.e_all[8 * b : 8 * b + 8, 32:64, :] = tdot(
            s.act[:, 256 * b : 256 * b + 256], s.ls[...]
        ).reshape(8, 32, C)
    s.e_all[:, 64:72, :] = tdot(s.spread[...], s.grh[...]).reshape(32, 8, C)
    e_core = remote(
        s.e_all.at[pl.ds((1 - c) * KXY, KXY)], s.e_core, s.e_cs.at[0], s.e_cs.at[1], other
    )
    e_core.start()
    b_middle()

    for r in range(0, ROWS, CH):
        rows = slice(r, r + CH)
        for g in range(2):
            s.ga[rows, 256 * g : 256 * g + 256] = dot(
                s.gspr[rows, 128 * g : 128 * g + 128],
                s.bdm[128 * g : 128 * g + 128, 256 * g : 256 * g + 256],
            )

    def scatter_xy(src, buf, sem):
        def put(i):
            xx, yy = at_xy(i)
            return remote(
                src.at[xx * NY + yy], buf.at[i], sem.at[0, i], sem.at[1, i], dev_xy(xx, yy)
            )

        def start():
            each(KXY - 1, lambda i: put(i).start())

        def wait():
            each(KXY - 1, lambda i: put(i).wait_recv())

        def drain():
            each(KXY - 1, lambda i: put(i).wait_send())

        return start, wait, drain

    def gather_xy(buf, sem):
        def put(i):
            return remote(
                buf.at[own], buf.at[own], sem.at[0, i], sem.at[1, i], dev_xy(*at_xy(i))
            )

        def got(i):
            xx, yy = from_xy(i)
            f = c * KXY + xx * NY + yy
            return remote(buf.at[f], buf.at[f], sem.at[0, i], sem.at[1, i], dev_xy(xx, yy))

        def start():
            each(KXY - 1, lambda i: put(i).start())

        def wait():
            each(KXY - 1, lambda i: got(i).wait_recv())

        def drain():
            each(KXY - 1, lambda i: put(i).wait_send())

        return start, wait, drain

    def gather_core(buf, sem):
        mine, theirs = pl.ds(c * KXY, KXY), pl.ds((1 - c) * KXY, KXY)
        put = remote(buf.at[mine], buf.at[mine], sem.at[0], sem.at[1], other)
        got = remote(buf.at[theirs], buf.at[theirs], sem.at[0], sem.at[1], other)
        return put.start, got.wait_recv, put.wait_send

    e_core.wait_recv()

    def add_core(i):
        s.e_core[i] = s.e_core[i] + s.e_all[c * KXY + i]

    each(KXY, add_core)
    ex_start, ex_wait, ex_drain = scatter_xy(s.e_core, s.e_xy, s.e_xys)
    ex_start()

    gm = b_finish()
    dv = hdot(gm, att, (1, 0))
    datt = hdot(gm, v, (0, 0))
    dsc = att * (datt - jnp.sum(att * datt, axis=-1, keepdims=True)) * HD ** (-0.5)
    dq = hdot(kk, dsc, (1, 1))
    dk = hdot(q, dsc, (1, 0))
    dqkv = jnp.concatenate([dq, dk, dv], axis=0)
    tokenmap = hdot(tokens, dqkv, (1, 1))
    dtok = hdot(wt, dqkv, (1, 0))
    gsum = dtok * inv_mass
    s.b_m[y, 0:HD, :] = gsum
    s.b_m[y, HD:, :] = jnp.broadcast_to(-jnp.sum(gsum * tokens, axis=0, keepdims=True), (8, 128))
    bm_start()
    bm_wait()
    for j in range(PAIRS):
        s.bdg[64 * j : 64 * j + 64, 128 * j : 128 * j + 128] = spread_diag(s.b_m[j, 0:HD, :])
    gmass = jnp.concatenate([s.b_m[j, HD : HD + 1, :] for j in range(PAIRS)], axis=1)

    for r in range(0, ROWS, CH):
        rows = slice(r, r + CH)
        ga = s.ga[rows, :] + gmass
        ga = ga + jnp.concatenate(
            [
                dot(
                    s.feat[rows, 128 * g : 128 * g + 128],
                    s.bdg[128 * g : 128 * g + 128, 256 * g : 256 * g + 256],
                )
                for g in range(2)
            ],
            axis=1,
        )
        a = s.asg[rows, :]
        gl = (a * (ga - seg_sum(a * ga, s.ones[...])) * inv_sharp).astype(BF16)
        s.gl[rows, :] = gl
        s.gp[rows, :] = jnp.concatenate(
            [
                dot_t(
                    gl[:, 256 * g : 256 * g + 256],
                    s.bdw[128 * g : 128 * g + 128, 256 * g : 256 * g + 256],
                )
                for g in range(2)
            ],
            axis=1,
        ).astype(BF16)
        s.gf[rows, :] = jnp.concatenate(
            [
                dot_t(
                    s.ah[rows, 256 * g : 256 * g + 256],
                    s.bdg[128 * g : 128 * g + 128, 256 * g : 256 * g + 256],
                )
                for g in range(2)
            ],
            axis=1,
        ).astype(BF16)

    s.l_all[:, 0:8, :] = tdot(s.nh[...], s.gf[...]).reshape(32, 8, C)
    s.l_all[:, 8:16, :] = tdot(s.nh[...], s.gp[...]).reshape(32, 8, C)
    slices = jnp.zeros((HD, 128), F32)
    for g in range(2):
        t = tdot(s.proj[:, 128 * g : 128 * g + 128], s.gl[:, 256 * g : 256 * g + 256])
        for j in range(2):
            slices = slices + pack_diag(t[64 * j : 64 * j + 64, 128 * j : 128 * j + 128])
    tokenmap = jnp.where(z == 0, tokenmap, jnp.zeros_like(tokenmap))
    small = jnp.concatenate([slices, tokenmap, jnp.zeros((HD, 32), F32)], axis=1)
    for i in range(32):
        s.l_all[i, 16:17, :] = small[i : i + 1, :]
    l_core = remote(
        s.l_all.at[pl.ds((1 - c) * KXY, KXY)], s.l_core, s.l_cs.at[0], s.l_cs.at[1], other
    )
    l_core.start()

    ex_wait()
    part = s.e_core[k]
    for i in range(KXY - 1):
        part = part + s.e_xy[i]
    s.e_part[...] = part

    def e_putz(i):
        t = at_z(i)
        return remote(
            s.e_part.at[pl.ds(pl.multiple_of(8 * t, 8), 8)],
            s.e_z.at[z],
            s.e_zs.at[0, i],
            s.e_zs.at[1, i],
            dev_z(t),
        )

    def e_gotz(i):
        f = from_z(i)
        return remote(s.e_z.at[f], s.e_z.at[f], s.e_zs.at[0, i], s.e_zs.at[1, i], dev_z(f))

    def e_putzo(i):
        return remote(
            s.e_part.at[pl.ds(64, 8)],
            s.e_zo.at[z],
            s.e_zos.at[0, i],
            s.e_zos.at[1, i],
            dev_z(at_z(i)),
        )

    def e_gotzo(i):
        f = from_z(i)
        return remote(s.e_zo.at[f], s.e_zo.at[f], s.e_zos.at[0, i], s.e_zos.at[1, i], dev_z(f))

    def e_startz(i):
        e_putz(i).start()
        e_putzo(i).start()

    each(NZ - 1, e_startz)
    s.e_z[z] = s.e_part[pl.ds(pl.multiple_of(8 * z, 8), 8), :]
    s.e_zo[z] = s.e_part[64:72, :]

    l_core.wait_recv()

    def add_core_late(i):
        s.l_core[i] = s.l_core[i] + s.l_all[c * KXY + i]

    each(KXY, add_core_late)
    lx_start, lx_wait, lx_drain = scatter_xy(s.l_core, s.l_xy, s.l_xys)
    lx_start()

    each(NZ - 1, lambda i: e_gotz(i).wait_recv())
    total = s.e_z[0]
    for i in range(1, NZ):
        total = total + s.e_z[i]
    myrows = pl.ds(pl.multiple_of(8 * z, 8), 8)
    s.e_fin[own, myrows, :] = total * scale

    def e_putzg(i):
        piece = s.e_fin.at[own, myrows]
        return remote(piece, piece, s.e_zgs.at[0, i], s.e_zgs.at[1, i], dev_z(at_z(i)))

    def e_gotzg(i):
        f = from_z(i)
        piece = s.e_fin.at[own, pl.ds(pl.multiple_of(8 * f, 8), 8)]
        return remote(piece, piece, s.e_zgs.at[0, i], s.e_zgs.at[1, i], dev_z(f))

    each(NZ - 1, lambda i: e_putzg(i).start())
    each(NZ - 1, lambda i: e_gotzo(i).wait_recv())
    total = s.e_zo[0]
    for i in range(1, NZ):
        total = total + s.e_zo[i]
    s.e_fin[own, 64:72, :] = total * scale

    lx_wait()
    part = s.l_core[k]
    for i in range(KXY - 1):
        part = part + s.l_xy[i]
    s.l_z[z] = part

    def l_putz(i):
        return remote(
            s.l_z.at[z], s.l_z.at[z], s.l_zs.at[0, i], s.l_zs.at[1, i], dev_z(at_z(i))
        )

    def l_gotz(i):
        f = from_z(i)
        return remote(s.l_z.at[f], s.l_z.at[f], s.l_zs.at[0, i], s.l_zs.at[1, i], dev_z(f))

    each(NZ - 1, lambda i: l_putz(i).start())

    each(NZ - 1, lambda i: e_gotzg(i).wait_recv())
    eg_start, eg_wait, eg_drain = gather_xy(s.e_fin, s.e_xygs)
    eg_start()

    for r in range(0, ROWS, CH):
        rows = slice(r, r + CH)
        normed, inv = norm_rows(s.mp[rows, :].astype(F32))
        gn = dot_t(s.gf[rows, :], s.wa[...]) + dot_t(s.gp[rows, :], s.wp[...])
        s.pgr[rows, :] = (s.gres[rows, :] + norm_back(normed, inv, gn)).astype(BF16)
    out_pg = pltpu.make_async_copy(s.pgr, o_pg, s.out_sem.at[1])
    out_pg.start()

    each(NZ - 1, lambda i: l_gotz(i).wait_recv())
    total = s.l_z[0]
    for i in range(1, NZ):
        total = total + s.l_z[i]
    s.l_fin[own] = total * scale
    lg_start, lg_wait, lg_drain = gather_xy(s.l_fin, s.l_xygs)
    lg_start()

    eg_wait()
    ec_start, ec_wait, ec_drain = gather_core(s.e_fin, s.e_cgs)
    ec_start()
    lg_wait()
    lc_start, lc_wait, lc_drain = gather_core(s.l_fin, s.l_cgs)
    lc_start()

    ec_wait()
    outs = [out_upd, out_pg]
    for b in range(4):
        outs.append(
            pltpu.make_async_copy(
                s.e_fin.at[:, pl.ds(8 * b, 8), :],
                o_up.at[:, :, pl.ds(256 * b, 256)],
                s.out_sem.at[2 + b],
            )
        )
    outs.append(pltpu.make_async_copy(s.e_fin.at[:, pl.ds(32, 32), :], o_down, s.out_sem.at[6]))
    outs.append(pltpu.make_async_copy(s.e_fin.at[:, pl.ds(64, 8), :], o_out, s.out_sem.at[7]))
    for o in outs[2:]:
        o.start()
    lc_wait()
    late = [
        pltpu.make_async_copy(s.l_fin.at[:, pl.ds(0, 8), :], o_feat, s.out_sem.at[8]),
        pltpu.make_async_copy(s.l_fin.at[:, pl.ds(8, 8), :], o_proj, s.out_sem.at[9]),
    ]
    for o in late:
        o.start()
    rows = [s.l_fin[i, 16:17, :] for i in range(32)]
    small = jnp.concatenate(rows, axis=0)
    o_slice[...] = small[:, 0:SL] + small[:, SL : 2 * SL]
    o_tok[...] = small[:, 128 : 128 + 3 * HD]

    a_drain()
    am_drain()
    b_drain()
    bm_drain()
    e_core.wait_send()
    ex_drain()
    l_core.wait_send()
    lx_drain()
    each(NZ - 1, lambda i: e_putz(i).wait_send())
    each(NZ - 1, lambda i: e_putzo(i).wait_send())
    each(NZ - 1, lambda i: e_putzg(i).wait_send())
    each(NZ - 1, lambda i: l_putz(i).wait_send())
    eg_drain()
    lg_drain()
    ec_drain()
    lc_drain()
    for o in outs + late:
        o.wait()


def body(mp, ls, wa, wp, ws, wt, wc, we, wd, sharp):
    scale = (lax.axis_size("dp") * lax.axis_size("point") * ROWS) ** (-0.5)
    anyspace = pl.BlockSpec(memory_space=pl.ANY)
    vmem = pl.BlockSpec(memory_space=pltpu.VMEM)
    outs = pl.pallas_call(
        functools.partial(kernel, scale),
        out_shape=(
            jax.ShapeDtypeStruct((ROWS, C), BF16),
            jax.ShapeDtypeStruct((ROWS, C), BF16),
            jax.ShapeDtypeStruct((32, 8, C), F32),
            jax.ShapeDtypeStruct((32, 8, C), F32),
            jax.ShapeDtypeStruct((HD, SL), F32),
            jax.ShapeDtypeStruct((HD, 3 * HD), F32),
            jax.ShapeDtypeStruct((32, 8, C), F32),
            jax.ShapeDtypeStruct((32, 8, FF), F32),
            jax.ShapeDtypeStruct((32, 32, C), F32),
        ),
        in_specs=[anyspace] * 9 + [pl.BlockSpec(memory_space=pltpu.SMEM)],
        out_specs=(anyspace,) * 4 + (vmem,) * 2 + (anyspace,) * 3,
        scratch_shapes=list(SCRATCH.values()),
        compiler_params=pltpu.CompilerParams(
            collective_id=0, has_side_effects=True, vmem_limit_bytes=48 << 20
        ),
        name="layer",
    )(mp[0], ls[0], wa, wp, ws, wt, wc, we, wd, sharp)
    upd, pg, feat, proj, sl, tok, out, up, down = outs
    return (
        upd[None],
        pg[None],
        feat.reshape(C, C),
        proj.reshape(C, C),
        sl,
        tok,
        out.reshape(C, C),
        up.reshape(C, FF),
        down.reshape(FF, C),
    )


def solution(mesh):
    split = P("dp", "point", None)
    return jax.shard_map(
        body,
        mesh=mesh,
        in_specs=(split, split) + (P(),) * 8,
        out_specs=(split, split) + (P(),) * 7,
        check_vma=False,
    )
```

time: 603 us -> 106 us (0.18)
  waiting for transfers between devices: 397 us -> 0 us
  blocking collectives: 143 us -> 0 us
  Pallas kernels: 0 us -> 89.8 us
  matrix products: 33 us -> 0 us
  between operations: 14.3 us -> 0.68 us
    psum x3 -> x0, waiting for transfers between devices: 397 us -> none  [the longest x1 184 us: body(): lax.psum((feature_term, project_term, slice_term, token_term, output_term...]
    psum x2 -> x0, blocking collectives: 143 us -> none  [the longest x1 78.5 us: body(): lax.psum((feature_term, project_term, slice_term, token_term, output_term...]
    pallas_call x0 -> x1, Pallas kernels: none -> 89.8 us  [body(): pl.pallas_call(functools.partial(kernel, scale), out_shape=(jax.ShapeDtyp...]
    dot_general x32 -> x0, matrix products: 31.5 us -> none  [the longest x3 3.85 us: token_mix(): jnp.einsum('vts,vzs->vtz', slice_query_rows, slice_key_rows, precision=la...]
    unnamed x67 -> x29, local copies, waits for them, and re-layouts: 13.2 us -> 15.4 us
  transfers between devices with their start and end apart: 3 -> 0, of which waited for: 3 -> 0; matrix products, arithmetic and copies ran while one was open for 1% -> 0% of each run, Pallas kernels for 0% -> 0%
where the time goes in v1:
time: 106 us
  Pallas kernels  89.8 us (85%)
  local copies, waits for them, and re-layouts  15.4 us (15%)
    pallas_call x1, Pallas kernels, body(): pl.pallas_call(functools.partial(kernel, scale), out_shape=(jax.ShapeDtyp...  89.8 us
    unnamed x29, local copies, waits for them, and re-layouts  15.4 us

profile of v1, /device:TPU:1, one launch (start us, length us, event | category | flops | bytes accessed | tf_op | source)
XLA Modules:
  0.0 105.8 jit_solution(4774670477695301854)
XLA Ops:
  0.6 0.0 copy-start.9
  0.7 0.6 copy-done.9
  1.3 0.0 copy-start
  1.3 1.0 copy-done
  2.3 0.0 copy-start.1
  2.3 1.0 copy-done.1
  3.4 0.0 copy-start.2
  3.4 0.9 copy-done.2
  4.3 0.0 copy-start.3
  4.3 0.9 copy-done.3
  5.3 0.0 copy-start.4
  5.3 0.9 copy-done.4
  6.2 0.0 copy-start.5
  6.2 0.9 copy-done.5
  7.1 0.0 copy-start.6
  7.1 0.9 copy-done.6
  8.0 0.0 copy-start.7
  8.0 0.7 copy-done.7
  8.7 0.0 copy-start.8
  8.7 0.7 copy-done.8
  9.4 89.8 %layer.1 = (bf16[512,256]{1,0:T(8,128)(2,1)S(1)}, bf16[512,256]{1,0:T(8,128)(2,1)S(1)}, f32[32,8,256]{2,1,0:T(8,128)S(1)}, f32[32,8,256]{2,1,0:T(8,128)S(1)}, f3...) custom-call(bf16[512,256]{1,0:T(8,128)(2,1)S(1)} %bitcast.11, ...), custom_call_target="tpu_custom_call" | custom-call | tf_op jit(solution)/shard_map/layer/pallas_call | solution.py:734
  99.2 0.7 copy.28
  99.9 0.7 copy.29
  100.6 0.7 copy.30
  101.3 0.7 copy.31
  102.0 0.6 copy.32
  102.6 0.6 copy.33
  103.2 0.7 copy.34
  103.9 1.0 copy.35
  104.9 1.0 copy.36
Async XLA Ops:
  0.6 0.7 copy-start.9
  1.3 1.0 copy-start
  2.3 1.0 copy-start.1
  3.4 0.9 copy-start.2
  4.3 0.9 copy-start.3
  5.3 0.9 copy-start.4
  6.2 0.9 copy-start.5
  7.1 0.9 copy-start.6
  8.0 0.7 copy-start.7
  8.7 0.7 copy-start.8

commit v2 on v1

--- a/solution.py
+++ b/solution.py
@@ -19,9 +19,9 @@
 C, FF, HEADS, HD, SL = 256, 1024, 8, 32, 64
 PAIRS = 4
 KXY = NX * NY
-EROWS = 72
+PARTS = ((16, 24), (16, 16))
 LROWS = 17
-CH = 128
+CH = 512
 
 
 def dot(a, b):
@@ -113,6 +113,9 @@
     gp=pltpu.VMEM((ROWS, C), BF16),
     upd=pltpu.VMEM((ROWS, C), BF16),
     pgr=pltpu.VMEM((ROWS, C), BF16),
+    slc=pltpu.VMEM((HD, SL), F32),
+    tok=pltpu.VMEM((HD, 3 * HD), F32),
+    out_sem=pltpu.SemaphoreType.DMA((13,)),
     a_p=pltpu.VMEM((PAIRS, 40, 128), F32),
     a_y=pltpu.VMEM((3, 40, 128), F32),
     a_z=pltpu.VMEM((NZ, 40, 128), F32),
@@ -127,20 +130,6 @@
     b_ys=pltpu.SemaphoreType.DMA((2, 3)),
     b_zs=pltpu.SemaphoreType.DMA((2, 7)),
     b_ms=pltpu.SemaphoreType.DMA((2, 3)),
-    e_all=pltpu.VMEM((2 * KXY, EROWS, C), F32),
-    e_core=pltpu.VMEM((KXY, EROWS, C), F32),
-    e_xy=pltpu.VMEM((KXY - 1, EROWS, C), F32),
-    e_part=pltpu.VMEM((EROWS, C), F32),
-    e_z=pltpu.VMEM((NZ, 8, C), F32),
-    e_zo=pltpu.VMEM((NZ, 8, C), F32),
-    e_fin=pltpu.VMEM((2 * KXY, EROWS, C), F32),
-    e_cs=pltpu.SemaphoreType.DMA((2,)),
-    e_xys=pltpu.SemaphoreType.DMA((2, KXY - 1)),
-    e_zs=pltpu.SemaphoreType.DMA((2, 7)),
-    e_zos=pltpu.SemaphoreType.DMA((2, 7)),
-    e_zgs=pltpu.SemaphoreType.DMA((2, 7)),
-    e_xygs=pltpu.SemaphoreType.DMA((2, KXY - 1)),
-    e_cgs=pltpu.SemaphoreType.DMA((2,)),
     l_all=pltpu.VMEM((2 * KXY, LROWS, C), F32),
     l_core=pltpu.VMEM((KXY, LROWS, C), F32),
     l_xy=pltpu.VMEM((KXY - 1, LROWS, C), F32),
@@ -151,12 +140,252 @@
     l_zs=pltpu.SemaphoreType.DMA((2, 7)),
     l_xygs=pltpu.SemaphoreType.DMA((2, KXY - 1)),
     l_cgs=pltpu.SemaphoreType.DMA((2,)),
-    out_sem=pltpu.SemaphoreType.DMA((10,)),
 )
+
+
+def early_scratch(p, ru, rv):
+    f = lambda *shape: pltpu.VMEM(shape + (C,), F32)
+    d = lambda *shape: pltpu.SemaphoreType.DMA((2,) + shape)
+    names = dict(
+        u=f(32, ru), v=f(32, rv), uc=f(KXY, ru), vc=f(KXY, rv),
+        ux=f(3, 4, ru), vy=f(3, 4, rv), u1=f(4, ru), v1=f(4, rv),
+        uy=f(3, ru), vx=f(3, rv), part=f(ru + rv),
+        z=pltpu.VMEM((NZ, 8, 128), F32), zo=f(NZ, 8), zf=f(32),
+        uf=f(32, ru), vf=f(32, rv),
+        us=d(4), vs=d(4), uxs=d(3), vys=d(3), uys=d(3), vxs=d(3),
+        zs=d(7), zos=d(7), zgs=d(7), uygs=d(3), vxgs=d(3), uxgs=d(3), vygs=d(3), ugs=d(4), vgs=d(4),
+    )
+    return {"e%d_%s" % (p, n): spec for n, spec in names.items()}
+
+
+for p, rows in enumerate(PARTS):
+    SCRATCH.update(early_scratch(p, *rows))
 
 
 class Names:
     pass
+
+
+class Axis:
+    def __init__(self, n, me, dev):
+        self.n, self.me, self.dev = n, me, dev
+
+    def to(self, i):
+        return lax.rem(self.me + i + 1, self.n)
+
+    def frm(self, i):
+        return lax.rem(self.me + self.n - 1 - i, self.n)
+
+
+class Early:
+    def __init__(self, s, p, rows, place, scale):
+        for name in early_scratch(0, 1, 1):
+            setattr(self, name[3:], getattr(s, "e%d_%s" % (p, name[3:])))
+        self.ru, self.rv = rows
+        self.out = self.rv > 16
+        self.scale = scale
+        x, c, z, y = place
+        self.x, self.c, self.pz, self.y = x, c, z, y
+        self.ax = Axis(NX, x, lambda t: (t * NC + c, z * NY + y))
+        self.ay = Axis(NY, y, lambda t: (x * NC + c, z * NY + t))
+        self.az = Axis(NZ, z, lambda t: (x * NC + c, t * NY + y))
+        self.other = (x * NC + (1 - c), z * NY + y)
+        self.first = ((self.ax, self.u, self.uc, self.ux, self.u1, self.us, self.uxs),
+                      (self.ay, self.v, self.vc, self.vy, self.v1, self.vs, self.vys))
+        self.second = ((self.ay, self.u1, self.uy, self.uys, 0, self.ru),
+                       (self.ax, self.v1, self.vx, self.vxs, self.ru, self.rv))
+        self.fin2 = ((self.ay, self.uf, 16 * c + 4 * x, self.uygs),
+                     (self.ax, self.vf, 16 * c + 4 * y, self.vxgs))
+        self.fin1 = ((self.ax, self.uf, self.uxgs, self.ugs), (self.ay, self.vf, self.vygs, self.vgs))
+        self.sent = []
+
+    def block(self, c, t):
+        return pl.ds(16 * c + 4 * t, 4)
+
+    def core_start(self):
+        for o in (0, 1, 2, 3):
+            for ax, full, half, _, _, sem, _ in self.first:
+                self.core_copy(ax, full, half, sem, o).start()
+
+    def core_copy(self, ax, full, half, sem, o):
+        t = lax.rem(ax.me + 1 + o, 4)
+        return remote(
+            full.at[self.block(1 - self.c, t)], half.at[pl.ds(4 * t, 4)], sem.at[0, o], sem.at[1, o],
+            self.other,
+        )
+
+    def st1_copy(self, ax, half, slots, sem, i):
+        t = ax.to(i)
+        return remote(half.at[pl.ds(4 * t, 4)], slots.at[i], sem.at[0, i], sem.at[1, i], ax.dev(t))
+
+    def st1_start(self):
+        for o in (0, 1, 2, 3):
+            for ax, full, half, slots, _, sem, sem1 in self.first:
+                self.core_copy(ax, full, half, sem, o).wait_recv()
+                t = lax.rem(ax.me + 1 + o, 4)
+                mine = pl.ds(4 * t, 4)
+                half[mine] = half[mine] + full[self.block(self.c, t)]
+                if o < 3:
+                    self.st1_copy(ax, half, slots, sem1, o).start()
+
+    def st2_copy(self, ax, src, slots, sem, i):
+        t = ax.to(i)
+        return remote(src.at[t], slots.at[i], sem.at[0, i], sem.at[1, i], ax.dev(t))
+
+    def st2_start(self):
+        for (ax, _, half, slots, one, _, sem1), (ax2, src, slots2, sem2, _, _) in zip(
+            self.first, self.second
+        ):
+            for i in range(3):
+                self.st1_copy(ax, half, slots, sem1, i).wait_recv()
+            one[...] = half[pl.ds(4 * ax.me, 4)] + slots[0] + slots[1] + slots[2]
+            for i in range(3):
+                self.st2_copy(ax2, src, slots2, sem2, i).start()
+
+    def tile(self, t):
+        return (
+            pl.ds(pl.multiple_of(8 * (t // 2), 8), 8),
+            pl.ds(pl.multiple_of(128 * (t % 2), 128), 128),
+        )
+
+    def z_copy(self, i):
+        t = self.az.to(i)
+        rows, lanes = self.tile(t)
+        return remote(
+            self.part.at[rows, lanes], self.z.at[self.pz], self.zs.at[0, i], self.zs.at[1, i],
+            self.az.dev(t),
+        )
+
+    def z_got(self, i):
+        f = self.az.frm(i)
+        return remote(
+            self.z.at[f], self.z.at[f], self.zs.at[0, i], self.zs.at[1, i], self.az.dev(f)
+        )
+
+    def zo_copy(self, i):
+        t = self.az.to(i)
+        return remote(
+            self.part.at[pl.ds(32, 8)], self.zo.at[self.pz], self.zos.at[0, i], self.zos.at[1, i],
+            self.az.dev(t),
+        )
+
+    def zo_got(self, i):
+        f = self.az.frm(i)
+        return remote(
+            self.zo.at[f], self.zo.at[f], self.zos.at[0, i], self.zos.at[1, i], self.az.dev(f)
+        )
+
+    def z_start(self):
+        for ax, src, slots, sem, at, n in self.second:
+            for i in range(3):
+                self.st2_copy(ax, src, slots, sem, i).wait_recv()
+            self.part[at : at + n, :] = src[ax.me] + slots[0] + slots[1] + slots[2]
+        each(7, lambda i: self.z_copy(i).start())
+        rows, lanes = self.tile(self.pz)
+        self.z[self.pz] = self.part[rows, lanes]
+        if self.out:
+            each(7, lambda i: self.zo_copy(i).start())
+            self.zo[self.pz] = self.part[32:40, :]
+
+    def zg_copy(self, i):
+        piece = self.zf.at[self.tile(self.pz)]
+        return remote(
+            piece, piece, self.zgs.at[0, i], self.zgs.at[1, i], self.az.dev(self.az.to(i))
+        )
+
+    def zg_got(self, i):
+        f = self.az.frm(i)
+        piece = self.zf.at[self.tile(f)]
+        return remote(piece, piece, self.zgs.at[0, i], self.zgs.at[1, i], self.az.dev(f))
+
+    def zg_start(self):
+        each(7, lambda i: self.z_got(i).wait_recv())
+        total = self.z[0]
+        for i in range(1, NZ):
+            total = total + self.z[i]
+        self.zf[self.tile(self.pz)] = total * self.scale
+        each(7, lambda i: self.zg_copy(i).start())
+
+    def fin2_copy(self, ax, fin, base, sem, i):
+        piece = fin.at[base + ax.me]
+        return remote(piece, piece, sem.at[0, i], sem.at[1, i], ax.dev(ax.to(i)))
+
+    def fin2_got(self, ax, fin, base, sem, i):
+        f = ax.frm(i)
+        piece = fin.at[base + f]
+        return remote(piece, piece, sem.at[0, i], sem.at[1, i], ax.dev(f))
+
+    def st2g_start(self):
+        own_u = 16 * self.c + 4 * self.x + self.y
+        own_v = 16 * self.c + 4 * self.y + self.x
+        if self.out:
+            each(7, lambda i: self.zo_got(i).wait_recv())
+            total = self.zo[0]
+            for i in range(1, NZ):
+                total = total + self.zo[i]
+            self.vf[own_v, 16:24, :] = total * self.scale
+        each(7, lambda i: self.zg_got(i).wait_recv())
+        self.uf[own_u] = self.zf[0:16, :]
+        self.vf[own_v, 0:16, :] = self.zf[16:32, :]
+        for ax, fin, base, sem in self.fin2:
+            for i in range(3):
+                self.fin2_copy(ax, fin, base, sem, i).start()
+
+    def fin1_copy(self, ax, fin, sem, i):
+        piece = fin.at[self.block(self.c, ax.me)]
+        return remote(piece, piece, sem.at[0, i], sem.at[1, i], ax.dev(ax.to(i)))
+
+    def fin1_got(self, ax, fin, sem, i):
+        f = ax.frm(i)
+        piece = fin.at[self.block(self.c, f)]
+        return remote(piece, piece, sem.at[0, i], sem.at[1, i], ax.dev(f))
+
+    def coreg_copy(self, ax, fin, sem, o):
+        piece = fin.at[self.block(self.c, lax.rem(ax.me + NX - o, 4))]
+        return remote(piece, piece, sem.at[0, o], sem.at[1, o], self.other)
+
+    def coreg_got(self, ax, fin, sem, o):
+        piece = fin.at[self.block(1 - self.c, lax.rem(ax.me + NX - o, 4))]
+        return remote(piece, piece, sem.at[0, o], sem.at[1, o], self.other)
+
+    def st1g_start(self):
+        for (ax2, fin, base, sem2), (ax, _, sem1, semc) in zip(self.fin2, self.fin1):
+            for i in range(3):
+                self.fin2_got(ax2, fin, base, sem2, i).wait_recv()
+            for i in range(3):
+                self.fin1_copy(ax, fin, sem1, i).start()
+            self.coreg_copy(ax, fin, semc, 0).start()
+
+    def coreg_start(self):
+        for i in (0, 2, 1):
+            for ax, fin, sem1, semc in self.fin1:
+                self.fin1_got(ax, fin, sem1, i).wait_recv()
+                self.coreg_copy(ax, fin, semc, i + 1).start()
+
+    def coreg_wait(self):
+        for ax, fin, _, semc in self.fin1:
+            for o in range(4):
+                self.coreg_got(ax, fin, semc, o).wait_recv()
+
+    def drain(self):
+        for (ax, full, half, slots, _, sem, sem1), (ax2, src, slots2, sem2, _, _) in zip(
+            self.first, self.second
+        ):
+            for o in range(4):
+                self.core_copy(ax, full, half, sem, o).wait_send()
+            for i in range(3):
+                self.st1_copy(ax, half, slots, sem1, i).wait_send()
+                self.st2_copy(ax2, src, slots2, sem2, i).wait_send()
+        each(7, lambda i: self.z_copy(i).wait_send())
+        each(7, lambda i: self.zg_copy(i).wait_send())
+        if self.out:
+            each(7, lambda i: self.zo_copy(i).wait_send())
+        for (ax2, fin, base, sem2), (ax, _, sem1, semc) in zip(self.fin2, self.fin1):
+            for i in range(3):
+                self.fin2_copy(ax2, fin, base, sem2, i).wait_send()
+                self.fin1_copy(ax, fin, sem1, i).wait_send()
+            for o in range(4):
+                self.coreg_copy(ax, fin, semc, o).wait_send()
 
 
 def kernel(scale, *refs):
@@ -192,6 +421,15 @@
     def from_xy(i):
         j = i + 1
         return lax.rem(x + NX - j // NY, NX), lax.rem(y + NY - j % NY, NY)
+
+    def at_x(i):
+        return lax.rem(x + i + 1, NX)
+
+    def from_x(i):
+        return lax.rem(x + NX - 1 - i, NX)
+
+    def dev_x(xx):
+        return (xx * NC + c, pt)
 
     def dev_y(yy):
         return (dp, z * NY + yy)
@@ -412,22 +650,28 @@
     b_start, b_middle, b_finish, b_drain = reduce_pairs(s.b_p, s.b_y, s.b_z, s.b_ys, s.b_zs)
     bm_start, bm_wait, bm_drain = gather_pairs(s.b_m, s.b_ms)
     b_start()
-    out_upd = pltpu.make_async_copy(s.upd, o_upd, s.out_sem.at[0])
-    out_upd.start()
-
-    for b in range(4):
-        s.e_all[:, 8 * b : 8 * b + 8, :] = tdot(
-            s.n2h[...], s.gh[:, 256 * b : 256 * b + 256]
-        ).reshape(32, 8, C)
-    for b in range(4):
-        s.e_all[8 * b : 8 * b + 8, 32:64, :] = tdot(
-            s.act[:, 256 * b : 256 * b + 256], s.ls[...]
-        ).reshape(8, 32, C)
-    s.e_all[:, 64:72, :] = tdot(s.spread[...], s.grh[...]).reshape(32, 8, C)
-    e_core = remote(
-        s.e_all.at[pl.ds((1 - c) * KXY, KXY)], s.e_core, s.e_cs.at[0], s.e_cs.at[1], other
-    )
-    e_core.start()
+    outs = []
+
+    def write(src, dst):
+        copy = pltpu.make_async_copy(src, dst, s.out_sem.at[len(outs)])
+        copy.start()
+        outs.append(copy)
+
+    write(s.upd, o_upd)
+
+    early = [Early(s, p, PARTS[p], (x, c, z, y), scale) for p in range(len(PARTS))]
+    for p, e in enumerate(early):
+        for b in range(2):
+            f = 256 * (2 * p + b)
+            e.u[:, 8 * b : 8 * b + 8, :] = tdot(s.n2h[...], s.gh[:, f : f + 256]).reshape(32, 8, C)
+            e.v[16 * b : 16 * b + 16, 0:16, :] = tdot(s.act[:, f : f + 256], s.ls[...]).reshape(
+                16, 16, C
+            )
+        if p == 0:
+            e.v[:, 16:24, :] = tdot(s.spread[...], s.grh[...]).reshape(32, 8, C)
+        e.core_start()
+    for e in early:
+        e.st1_start()
     b_middle()
 
     for r in range(0, ROWS, CH):
@@ -483,15 +727,6 @@
         put = remote(buf.at[mine], buf.at[mine], sem.at[0], sem.at[1], other)
         got = remote(buf.at[theirs], buf.at[theirs], sem.at[0], sem.at[1], other)
         return put.start, got.wait_recv, put.wait_send
-
-    e_core.wait_recv()
-
-    def add_core(i):
-        s.e_core[i] = s.e_core[i] + s.e_all[c * KXY + i]
-
-    each(KXY, add_core)
-    ex_start, ex_wait, ex_drain = scatter_xy(s.e_core, s.e_xy, s.e_xys)
-    ex_start()
 
     gm = b_finish()
     dv = hdot(gm, att, (1, 0))
@@ -506,6 +741,8 @@
     s.b_m[y, 0:HD, :] = gsum
     s.b_m[y, HD:, :] = jnp.broadcast_to(-jnp.sum(gsum * tokens, axis=0, keepdims=True), (8, 128))
     bm_start()
+    for e in early:
+        e.st2_start()
     bm_wait()
     for j in range(PAIRS):
         s.bdg[64 * j : 64 * j + 64, 128 * j : 128 * j + 128] = spread_diag(s.b_m[j, 0:HD, :])
@@ -564,47 +801,6 @@
     )
     l_core.start()
 
-    ex_wait()
-    part = s.e_core[k]
-    for i in range(KXY - 1):
-        part = part + s.e_xy[i]
-    s.e_part[...] = part
-
-    def e_putz(i):
-        t = at_z(i)
-        return remote(
-            s.e_part.at[pl.ds(pl.multiple_of(8 * t, 8), 8)],
-            s.e_z.at[z],
-            s.e_zs.at[0, i],
-            s.e_zs.at[1, i],
-            dev_z(t),
-        )
-
-    def e_gotz(i):
-        f = from_z(i)
-        return remote(s.e_z.at[f], s.e_z.at[f], s.e_zs.at[0, i], s.e_zs.at[1, i], dev_z(f))
-
-    def e_putzo(i):
-        return remote(
-            s.e_part.at[pl.ds(64, 8)],
-            s.e_zo.at[z],
-            s.e_zos.at[0, i],
-            s.e_zos.at[1, i],
-            dev_z(at_z(i)),
-        )
-
-    def e_gotzo(i):
-        f = from_z(i)
-        return remote(s.e_zo.at[f], s.e_zo.at[f], s.e_zos.at[0, i], s.e_zos.at[1, i], dev_z(f))
-
-    def e_startz(i):
-        e_putz(i).start()
-        e_putzo(i).start()
-
-    each(NZ - 1, e_startz)
-    s.e_z[z] = s.e_part[pl.ds(pl.multiple_of(8 * z, 8), 8), :]
-    s.e_zo[z] = s.e_part[64:72, :]
-
     l_core.wait_recv()
 
     def add_core_late(i):
@@ -614,28 +810,18 @@
     lx_start, lx_wait, lx_drain = scatter_xy(s.l_core, s.l_xy, s.l_xys)
     lx_start()
 
-    each(NZ - 1, lambda i: e_gotz(i).wait_recv())
-    total = s.e_z[0]
-    for i in range(1, NZ):
-        total = total + s.e_z[i]
-    myrows = pl.ds(pl.multiple_of(8 * z, 8), 8)
-    s.e_fin[own, myrows, :] = total * scale
-
-    def e_putzg(i):
-        piece = s.e_fin.at[own, myrows]
-        return remote(piece, piece, s.e_zgs.at[0, i], s.e_zgs.at[1, i], dev_z(at_z(i)))
-
-    def e_gotzg(i):
-        f = from_z(i)
-        piece = s.e_fin.at[own, pl.ds(pl.multiple_of(8 * f, 8), 8)]
-        return remote(piece, piece, s.e_zgs.at[0, i], s.e_zgs.at[1, i], dev_z(f))
-
-    each(NZ - 1, lambda i: e_putzg(i).start())
-    each(NZ - 1, lambda i: e_gotzo(i).wait_recv())
-    total = s.e_zo[0]
-    for i in range(1, NZ):
-        total = total + s.e_zo[i]
-    s.e_fin[own, 64:72, :] = total * scale
+    for e in early:
+        e.z_start()
+
+    for r in range(0, ROWS, CH):
+        rows = slice(r, r + CH)
+        normed, inv = norm_rows(s.mp[rows, :].astype(F32))
+        gn = dot_t(s.gf[rows, :], s.wa[...]) + dot_t(s.gp[rows, :], s.wp[...])
+        s.pgr[rows, :] = (s.gres[rows, :] + norm_back(normed, inv, gn)).astype(BF16)
+    write(s.pgr, o_pg)
+
+    for e in early:
+        e.zg_start()
 
     lx_wait()
     part = s.l_core[k]
@@ -654,18 +840,8 @@
 
     each(NZ - 1, lambda i: l_putz(i).start())
 
-    each(NZ - 1, lambda i: e_gotzg(i).wait_recv())
-    eg_start, eg_wait, eg_drain = gather_xy(s.e_fin, s.e_xygs)
-    eg_start()
-
-    for r in range(0, ROWS, CH):
-        rows = slice(r, r + CH)
-        normed, inv = norm_rows(s.mp[rows, :].astype(F32))
-        gn = dot_t(s.gf[rows, :], s.wa[...]) + dot_t(s.gp[rows, :], s.wp[...])
-        s.pgr[rows, :] = (s.gres[rows, :] + norm_back(normed, inv, gn)).astype(BF16)
-    out_pg = pltpu.make_async_copy(s.pgr, o_pg, s.out_sem.at[1])
-    out_pg.start()
-
+    for e in early:
+        e.st2g_start()
     each(NZ - 1, lambda i: l_gotz(i).wait_recv())
     total = s.l_z[0]
     for i in range(1, NZ):
@@ -674,84 +850,96 @@
     lg_start, lg_wait, lg_drain = gather_xy(s.l_fin, s.l_xygs)
     lg_start()
 
-    eg_wait()
-    ec_start, ec_wait, ec_drain = gather_core(s.e_fin, s.e_cgs)
-    ec_start()
+    for e in early:
+        e.st1g_start()
+    early[0].coreg_start()
     lg_wait()
     lc_start, lc_wait, lc_drain = gather_core(s.l_fin, s.l_cgs)
     lc_start()
-
-    ec_wait()
-    outs = [out_upd, out_pg]
-    for b in range(4):
-        outs.append(
-            pltpu.make_async_copy(
-                s.e_fin.at[:, pl.ds(8 * b, 8), :],
-                o_up.at[:, :, pl.ds(256 * b, 256)],
-                s.out_sem.at[2 + b],
+    for e in early[1:]:
+        e.coreg_start()
+    for p, e in enumerate(early):
+        e.coreg_wait()
+        for b in range(2):
+            write(
+                e.uf.at[:, pl.ds(8 * b, 8), :], o_up.at[:, :, pl.ds(256 * (2 * p + b), 256)]
             )
-        )
-    outs.append(pltpu.make_async_copy(s.e_fin.at[:, pl.ds(32, 32), :], o_down, s.out_sem.at[6]))
-    outs.append(pltpu.make_async_copy(s.e_fin.at[:, pl.ds(64, 8), :], o_out, s.out_sem.at[7]))
-    for o in outs[2:]:
-        o.start()
+        write(e.vf.at[:, pl.ds(0, 16), :], o_down.at[pl.ds(32 * p, 32)])
+        if p == 0:
+            write(e.vf.at[:, pl.ds(16, 8), :], o_out)
     lc_wait()
-    late = [
-        pltpu.make_async_copy(s.l_fin.at[:, pl.ds(0, 8), :], o_feat, s.out_sem.at[8]),
-        pltpu.make_async_copy(s.l_fin.at[:, pl.ds(8, 8), :], o_proj, s.out_sem.at[9]),
-    ]
-    for o in late:
-        o.start()
+    write(s.l_fin.at[:, pl.ds(0, 8), :], o_feat)
+    write(s.l_fin.at[:, pl.ds(8, 8), :], o_proj)
     rows = [s.l_fin[i, 16:17, :] for i in range(32)]
     small = jnp.concatenate(rows, axis=0)
-    o_slice[...] = small[:, 0:SL] + small[:, SL : 2 * SL]
-    o_tok[...] = small[:, 128 : 128 + 3 * HD]
+    s.slc[...] = small[:, 0:SL] + small[:, SL : 2 * SL]
+    s.tok[...] = small[:, 128 : 128 + 3 * HD]
+    write(s.slc, o_slice)
+    write(s.tok, o_tok)
 
     a_drain()
     am_drain()
     b_drain()
     bm_drain()
-    e_core.wait_send()
-    ex_drain()
     l_core.wait_send()
     lx_drain()
-    each(NZ - 1, lambda i: e_putz(i).wait_send())
-    each(NZ - 1, lambda i: e_putzo(i).wait_send())
-    each(NZ - 1, lambda i: e_putzg(i).wait_send())
     each(NZ - 1, lambda i: l_putz(i).wait_send())
-    eg_drain()
     lg_drain()
-    ec_drain()
     lc_drain()
-    for o in outs + late:
-        o.wait()
+    for e in early:
+        e.drain()
+    for copy in outs:
+        copy.wait()
+
+
+def store(*refs):
+    held, outs, stage, sem = refs[:9], refs[9:18], refs[18:27], refs[27]
+    loads = [pltpu.make_async_copy(held[i], stage[i], sem.at[0, i]) for i in range(9)]
+    stores = [pltpu.make_async_copy(stage[i], outs[i], sem.at[1, i]) for i in range(9)]
+    for copy in loads:
+        copy.start()
+    for i in range(9):
+        loads[i].wait()
+        stores[i].start()
+    for copy in stores:
+        copy.wait()
 
 
 def body(mp, ls, wa, wp, ws, wt, wc, we, wd, sharp):
     scale = (lax.axis_size("dp") * lax.axis_size("point") * ROWS) ** (-0.5)
-    anyspace = pl.BlockSpec(memory_space=pl.ANY)
-    vmem = pl.BlockSpec(memory_space=pltpu.VMEM)
-    outs = pl.pallas_call(
+    hbm = pl.BlockSpec(memory_space=pltpu.HBM)
+    results = (
+        jax.ShapeDtypeStruct((ROWS, C), BF16),
+        jax.ShapeDtypeStruct((ROWS, C), BF16),
+        jax.ShapeDtypeStruct((32, 8, C), F32),
+        jax.ShapeDtypeStruct((32, 8, C), F32),
+        jax.ShapeDtypeStruct((HD, SL), F32),
+        jax.ShapeDtypeStruct((HD, 3 * HD), F32),
+        jax.ShapeDtypeStruct((32, 8, C), F32),
+        jax.ShapeDtypeStruct((32, 8, FF), F32),
+        jax.ShapeDtypeStruct((64, 16, C), F32),
+    )
+    held = pl.pallas_call(
         functools.partial(kernel, scale),
-        out_shape=(
-            jax.ShapeDtypeStruct((ROWS, C), BF16),
-            jax.ShapeDtypeStruct((ROWS, C), BF16),
-            jax.ShapeDtypeStruct((32, 8, C), F32),
-            jax.ShapeDtypeStruct((32, 8, C), F32),
-            jax.ShapeDtypeStruct((HD, SL), F32),
-            jax.ShapeDtypeStruct((HD, 3 * HD), F32),
-            jax.ShapeDtypeStruct((32, 8, C), F32),
-            jax.ShapeDtypeStruct((32, 8, FF), F32),
-            jax.ShapeDtypeStruct((32, 32, C), F32),
-        ),
-        in_specs=[anyspace] * 9 + [pl.BlockSpec(memory_space=pltpu.SMEM)],
-        out_specs=(anyspace,) * 4 + (vmem,) * 2 + (anyspace,) * 3,
+        out_shape=results,
+        in_specs=[hbm] * 9 + [pl.BlockSpec(memory_space=pltpu.SMEM)],
+        out_specs=(hbm,) * 9,
         scratch_shapes=list(SCRATCH.values()),
         compiler_params=pltpu.CompilerParams(
-            collective_id=0, has_side_effects=True, vmem_limit_bytes=48 << 20
+            collective_id=0, has_side_effects=True, vmem_limit_bytes=58 << 20
         ),
         name="layer",
     )(mp[0], ls[0], wa, wp, ws, wt, wc, we, wd, sharp)
+    outs = pl.pallas_call(
+        store,
+        out_shape=results,
+        in_specs=[hbm] * 9,
+        out_specs=(hbm,) * 9,
+        scratch_shapes=[pltpu.VMEM(r.shape, r.dtype) for r in results]
+        + [pltpu.SemaphoreType.DMA((2, 9))],
+        compiler_params=pltpu.CompilerParams(vmem_limit_bytes=58 << 20),
+        name="store",
+    )(*held)
     upd, pg, feat, proj, sl, tok, out, up, down = outs
     return (
         upd[None],

time: 106 us -> 85.4 us (0.81)
  local copies, waits for them, and re-layouts: 15.4 us -> 0 us
  Pallas kernels: 89.8 us -> 84.6 us
    unnamed x29 -> x0, local copies, waits for them, and re-layouts: 15.4 us -> none
    pallas_call x1 -> x2, Pallas kernels: 89.8 us -> 84.6 us  [the longest x1 81.3 us: body(): pl.pallas_call(functools.partial(kernel, scale), out_shape=results, in_sp...]
where the time goes in v2:
time: 85.4 us; the launch traced here: 85.2 us
  Pallas kernels  84.6 us (99%)
    pallas_call x1, Pallas kernels, body(): pl.pallas_call(functools.partial(kernel, scale), out_shape=results, in_sp...  81.3 us
    pallas_call x1, Pallas kernels, body(): pl.pallas_call(store, out_shape=results, in_specs=[hbm] * 9, out_specs=(h...  3.33 us

profile of v2, /device:TPU:1, one launch (start us, length us, event | category | flops | bytes accessed | tf_op | source)
XLA Modules:
  0.0 85.2 jit_solution(3089593683272192370)
XLA Ops:
  0.6 81.3 %layer.1 = (bf16[512,256]{1,0:T(8,128)(2,1)}, bf16[512,256]{1,0:T(8,128)(2,1)}, f32[32,8,256]{2,1,0:T(8,128)}, f32[32,8,256]{2,1,0:T(8,128)}, f32[32,64]{1,0:T(8...) custom-call(bf16[512,256]{1,0:T(8,128)(2,1)} %bitcast.9, ...), custom_call_target="tpu_custom_call" | custom-call | tf_op jit(solution)/shard_map/layer/pallas_call | solution.py:922
  81.9 3.3 %store.1 = (bf16[512,256]{1,0:T(8,128)(2,1)}, bf16[512,256]{1,0:T(8,128)(2,1)}, f32[32,8,256]{2,1,0:T(8,128)}, f32[32,8,256]{2,1,0:T(8,128)}, f32[32,64]{1,0:T(8...) custom-call(bf16[512,256]{1,0:T(8,128)(2,1)} %get-tuple-element.27.refs_0_, ...), custom_call_target="tpu_custom_call" | custom-call | tf_op jit(solution)/shard_map/store/pallas_call | solution.py:933

commit v3 on v2

--- a/solution.py
+++ b/solution.py
@@ -20,7 +20,7 @@
 PAIRS = 4
 KXY = NX * NY
 PARTS = ((16, 24), (16, 16))
-LROWS = 17
+LATE = (8, 9)
 CH = 512
 
 
@@ -67,17 +67,19 @@
 
 
 def each(n, f):
-    def step(i, carry):
+    for i in range(n):
         f(i)
-        return carry
-
-    lax.fori_loop(0, n, step, 0)
 
 
 def remote(src, dst, ss, rs, dev):
     return pltpu.make_async_remote_copy(
         src_ref=src, dst_ref=dst, send_sem=ss, recv_sem=rs, device_id=dev, device_id_type=MESH
     )
+
+
+def whole(ref, sem, n, dev):
+    part = ref.at[pl.ds(0, n)]
+    return remote(part, part, sem.at[0], sem.at[1], dev)
 
 
 SCRATCH = dict(
@@ -116,30 +118,20 @@
     slc=pltpu.VMEM((HD, SL), F32),
     tok=pltpu.VMEM((HD, 3 * HD), F32),
     out_sem=pltpu.SemaphoreType.DMA((13,)),
-    a_p=pltpu.VMEM((PAIRS, 40, 128), F32),
-    a_y=pltpu.VMEM((3, 40, 128), F32),
-    a_z=pltpu.VMEM((NZ, 40, 128), F32),
+    a_p=pltpu.VMEM((PAIRS, 33, 128), F32),
+    a_y=pltpu.VMEM((3, 33, 128), F32),
+    a_z=pltpu.VMEM((NZ, 33, 128), F32),
     a_m=pltpu.VMEM((PAIRS, HD, 128), F32),
-    a_ys=pltpu.SemaphoreType.DMA((2, 3)),
-    a_zs=pltpu.SemaphoreType.DMA((2, 7)),
-    a_ms=pltpu.SemaphoreType.DMA((2, 3)),
+    a_ys=pltpu.SemaphoreType.DMA((2,)),
+    a_zs=pltpu.SemaphoreType.DMA((2,)),
+    a_ms=pltpu.SemaphoreType.DMA((2,)),
     b_p=pltpu.VMEM((PAIRS, HD, 128), F32),
     b_y=pltpu.VMEM((3, HD, 128), F32),
     b_z=pltpu.VMEM((NZ, HD, 128), F32),
-    b_m=pltpu.VMEM((PAIRS, 40, 128), F32),
-    b_ys=pltpu.SemaphoreType.DMA((2, 3)),
-    b_zs=pltpu.SemaphoreType.DMA((2, 7)),
-    b_ms=pltpu.SemaphoreType.DMA((2, 3)),
-    l_all=pltpu.VMEM((2 * KXY, LROWS, C), F32),
-    l_core=pltpu.VMEM((KXY, LROWS, C), F32),
-    l_xy=pltpu.VMEM((KXY - 1, LROWS, C), F32),
-    l_z=pltpu.VMEM((NZ, LROWS, C), F32),
-    l_fin=pltpu.VMEM((2 * KXY, LROWS, C), F32),
-    l_cs=pltpu.SemaphoreType.DMA((2,)),
-    l_xys=pltpu.SemaphoreType.DMA((2, KXY - 1)),
-    l_zs=pltpu.SemaphoreType.DMA((2, 7)),
-    l_xygs=pltpu.SemaphoreType.DMA((2, KXY - 1)),
-    l_cgs=pltpu.SemaphoreType.DMA((2,)),
+    b_m=pltpu.VMEM((PAIRS, 33, 128), F32),
+    b_ys=pltpu.SemaphoreType.DMA((2,)),
+    b_zs=pltpu.SemaphoreType.DMA((2,)),
+    b_ms=pltpu.SemaphoreType.DMA((2,)),
 )
 
 
@@ -152,12 +144,24 @@
         uy=f(3, ru), vx=f(3, rv), part=f(ru + rv),
         z=pltpu.VMEM((NZ, 8, 128), F32), zo=f(NZ, 8), zf=f(32),
         uf=f(32, ru), vf=f(32, rv),
-        us=d(4), vs=d(4), uxs=d(3), vys=d(3), uys=d(3), vxs=d(3),
-        zs=d(7), zos=d(7), zgs=d(7), uygs=d(3), vxgs=d(3), uxgs=d(3), vygs=d(3), ugs=d(4), vgs=d(4),
+        us=d(4), vs=d(4), uxs=d(), vys=d(), uys=d(), vxs=d(),
+        zs=d(), zos=d(), zgs=d(), uygs=d(), vxgs=d(), uxgs=d(3), vygs=d(3), ugs=d(4), vgs=d(4),
     )
     return {"e%d_%s" % (p, n): spec for n, spec in names.items()}
 
 
+def late_scratch(p, r):
+    f = lambda *shape: pltpu.VMEM(shape + (r, C), F32)
+    d = lambda *shape: pltpu.SemaphoreType.DMA((2,) + shape)
+    names = dict(
+        all=f(32), half=f(KXY), xy=f(KXY - 1), z=f(NZ), fin=f(32),
+        cs=d(), xys=d(), zs=d(), gs=d(), cgs=d(),
+    )
+    return {"l%d_%s" % (p, n): spec for n, spec in names.items()}
+
+
+for p, rows in enumerate(LATE):
+    SCRATCH.update(late_scratch(p, rows))
 for p, rows in enumerate(PARTS):
     SCRATCH.update(early_scratch(p, *rows))
 
@@ -216,7 +220,7 @@
 
     def st1_copy(self, ax, half, slots, sem, i):
         t = ax.to(i)
-        return remote(half.at[pl.ds(4 * t, 4)], slots.at[i], sem.at[0, i], sem.at[1, i], ax.dev(t))
+        return remote(half.at[pl.ds(4 * t, 4)], slots.at[i], sem.at[0], sem.at[1], ax.dev(t))
 
     def st1_start(self):
         for o in (0, 1, 2, 3):
@@ -230,14 +234,13 @@
 
     def st2_copy(self, ax, src, slots, sem, i):
         t = ax.to(i)
-        return remote(src.at[t], slots.at[i], sem.at[0, i], sem.at[1, i], ax.dev(t))
+        return remote(src.at[t], slots.at[i], sem.at[0], sem.at[1], ax.dev(t))
 
     def st2_start(self):
         for (ax, _, half, slots, one, _, sem1), (ax2, src, slots2, sem2, _, _) in zip(
             self.first, self.second
         ):
-            for i in range(3):
-                self.st1_copy(ax, half, slots, sem1, i).wait_recv()
+            whole(slots, sem1, 3, self.other).wait_recv()
             one[...] = half[pl.ds(4 * ax.me, 4)] + slots[0] + slots[1] + slots[2]
             for i in range(3):
                 self.st2_copy(ax2, src, slots2, sem2, i).start()
@@ -252,33 +255,20 @@
         t = self.az.to(i)
         rows, lanes = self.tile(t)
         return remote(
-            self.part.at[rows, lanes], self.z.at[self.pz], self.zs.at[0, i], self.zs.at[1, i],
+            self.part.at[rows, lanes], self.z.at[self.pz], self.zs.at[0], self.zs.at[1],
             self.az.dev(t),
-        )
-
-    def z_got(self, i):
-        f = self.az.frm(i)
-        return remote(
-            self.z.at[f], self.z.at[f], self.zs.at[0, i], self.zs.at[1, i], self.az.dev(f)
         )
 
     def zo_copy(self, i):
         t = self.az.to(i)
         return remote(
-            self.part.at[pl.ds(32, 8)], self.zo.at[self.pz], self.zos.at[0, i], self.zos.at[1, i],
+            self.part.at[pl.ds(32, 8)], self.zo.at[self.pz], self.zos.at[0], self.zos.at[1],
             self.az.dev(t),
         )
 
-    def zo_got(self, i):
-        f = self.az.frm(i)
-        return remote(
-            self.zo.at[f], self.zo.at[f], self.zos.at[0, i], self.zos.at[1, i], self.az.dev(f)
-        )
-
     def z_start(self):
         for ax, src, slots, sem, at, n in self.second:
-            for i in range(3):
-                self.st2_copy(ax, src, slots, sem, i).wait_recv()
+            whole(slots, sem, 3, self.other).wait_recv()
             self.part[at : at + n, :] = src[ax.me] + slots[0] + slots[1] + slots[2]
         each(7, lambda i: self.z_copy(i).start())
         rows, lanes = self.tile(self.pz)
@@ -290,16 +280,11 @@
     def zg_copy(self, i):
         piece = self.zf.at[self.tile(self.pz)]
         return remote(
-            piece, piece, self.zgs.at[0, i], self.zgs.at[1, i], self.az.dev(self.az.to(i))
+            piece, piece, self.zgs.at[0], self.zgs.at[1], self.az.dev(self.az.to(i))
         )
 
-    def zg_got(self, i):
-        f = self.az.frm(i)
-        piece = self.zf.at[self.tile(f)]
-        return remote(piece, piece, self.zgs.at[0, i], self.zgs.at[1, i], self.az.dev(f))
-
     def zg_start(self):
-        each(7, lambda i: self.z_got(i).wait_recv())
+        whole(self.z, self.zs, 7, self.other).wait_recv()
         total = self.z[0]
         for i in range(1, NZ):
             total = total + self.z[i]
@@ -308,23 +293,18 @@
 
     def fin2_copy(self, ax, fin, base, sem, i):
         piece = fin.at[base + ax.me]
-        return remote(piece, piece, sem.at[0, i], sem.at[1, i], ax.dev(ax.to(i)))
-
-    def fin2_got(self, ax, fin, base, sem, i):
-        f = ax.frm(i)
-        piece = fin.at[base + f]
-        return remote(piece, piece, sem.at[0, i], sem.at[1, i], ax.dev(f))
+        return remote(piece, piece, sem.at[0], sem.at[1], ax.dev(ax.to(i)))
 
     def st2g_start(self):
         own_u = 16 * self.c + 4 * self.x + self.y
         own_v = 16 * self.c + 4 * self.y + self.x
         if self.out:
-            each(7, lambda i: self.zo_got(i).wait_recv())
+            whole(self.zo, self.zos, 7, self.other).wait_recv()
             total = self.zo[0]
             for i in range(1, NZ):
                 total = total + self.zo[i]
             self.vf[own_v, 16:24, :] = total * self.scale
-        each(7, lambda i: self.zg_got(i).wait_recv())
+        whole(self.z, self.zgs, 7, self.other).wait_recv()
         self.uf[own_u] = self.zf[0:16, :]
         self.vf[own_v, 0:16, :] = self.zf[16:32, :]
         for ax, fin, base, sem in self.fin2:
@@ -350,8 +330,7 @@
 
     def st1g_start(self):
         for (ax2, fin, base, sem2), (ax, _, sem1, semc) in zip(self.fin2, self.fin1):
-            for i in range(3):
-                self.fin2_got(ax2, fin, base, sem2, i).wait_recv()
+            whole(fin, sem2, 3, self.other).wait_recv()
             for i in range(3):
                 self.fin1_copy(ax, fin, sem1, i).start()
             self.coreg_copy(ax, fin, semc, 0).start()
@@ -367,25 +346,111 @@
             for o in range(4):
                 self.coreg_got(ax, fin, semc, o).wait_recv()
 
-    def drain(self):
-        for (ax, full, half, slots, _, sem, sem1), (ax2, src, slots2, sem2, _, _) in zip(
+    def drain_sums(self):
+        for (ax, full, half, slots, _, sem, sem1), (_, _, slots2, sem2, _, _) in zip(
             self.first, self.second
         ):
             for o in range(4):
                 self.core_copy(ax, full, half, sem, o).wait_send()
+            whole(slots, sem1, 3, self.other).wait_send()
+            whole(slots2, sem2, 3, self.other).wait_send()
+
+    def drain(self):
+        whole(self.z, self.zs, 7, self.other).wait_send()
+        whole(self.z, self.zgs, 7, self.other).wait_send()
+        if self.out:
+            whole(self.zo, self.zos, 7, self.other).wait_send()
+        for (_, fin, _, sem2), (ax, _, sem1, semc) in zip(self.fin2, self.fin1):
+            whole(fin, sem2, 3, self.other).wait_send()
             for i in range(3):
-                self.st1_copy(ax, half, slots, sem1, i).wait_send()
-                self.st2_copy(ax2, src, slots2, sem2, i).wait_send()
-        each(7, lambda i: self.z_copy(i).wait_send())
-        each(7, lambda i: self.zg_copy(i).wait_send())
-        if self.out:
-            each(7, lambda i: self.zo_copy(i).wait_send())
-        for (ax2, fin, base, sem2), (ax, _, sem1, semc) in zip(self.fin2, self.fin1):
-            for i in range(3):
-                self.fin2_copy(ax2, fin, base, sem2, i).wait_send()
                 self.fin1_copy(ax, fin, sem1, i).wait_send()
             for o in range(4):
                 self.coreg_copy(ax, fin, semc, o).wait_send()
+
+
+class Late:
+    def __init__(self, s, p, place, scale):
+        for name in late_scratch(0, 1):
+            setattr(self, name[3:], getattr(s, "l%d_%s" % (p, name[3:])))
+        self.scale = scale
+        x, c, z, y = place
+        self.x, self.c, self.pz, self.y = x, c, z, y
+        self.k = x * NY + y
+        self.own = c * KXY + self.k
+        self.az = Axis(NZ, z, lambda t: (x * NC + c, t * NY + y))
+        self.other = (x * NC + (1 - c), z * NY + y)
+
+    def dev(self, xx, yy):
+        return (xx * NC + self.c, self.pz * NY + yy)
+
+    def to(self, i):
+        j = i + 1
+        return lax.rem(self.x + j // NY, NX), lax.rem(self.y + j % NY, NY)
+
+    def core_copy(self):
+        theirs = pl.ds((1 - self.c) * KXY, KXY)
+        return remote(self.all.at[theirs], self.half, self.cs.at[0], self.cs.at[1], self.other)
+
+    def core_start(self):
+        self.core_copy().start()
+
+    def xy_copy(self, i):
+        xx, yy = self.to(i)
+        return remote(
+            self.half.at[xx * NY + yy], self.xy.at[i], self.xys.at[0], self.xys.at[1],
+            self.dev(xx, yy),
+        )
+
+    def xy_start(self):
+        self.core_copy().wait_recv()
+        self.half[...] = self.half[...] + self.all[pl.ds(self.c * KXY, KXY)]
+        each(KXY - 1, lambda i: self.xy_copy(i).start())
+
+    def z_copy(self, i):
+        piece = self.z.at[self.pz]
+        return remote(
+            piece, piece, self.zs.at[0], self.zs.at[1], self.az.dev(self.az.to(i))
+        )
+
+    def z_start(self):
+        whole(self.xy, self.xys, KXY - 1, self.other).wait_recv()
+        part = self.half[self.k]
+        for i in range(KXY - 1):
+            part = part + self.xy[i]
+        self.z[self.pz] = part
+        each(NZ - 1, lambda i: self.z_copy(i).start())
+
+    def g_copy(self, i):
+        piece = self.fin.at[self.own]
+        return remote(piece, piece, self.gs.at[0], self.gs.at[1], self.dev(*self.to(i)))
+
+    def g_start(self):
+        whole(self.z, self.zs, NZ - 1, self.other).wait_recv()
+        total = self.z[0]
+        for i in range(1, NZ):
+            total = total + self.z[i]
+        self.fin[self.own] = total * self.scale
+        each(KXY - 1, lambda i: self.g_copy(i).start())
+
+    def c_copy(self, c):
+        mine = self.fin.at[pl.ds(c * KXY, KXY)]
+        return remote(mine, mine, self.cgs.at[0], self.cgs.at[1], self.other)
+
+    def c_start(self):
+        whole(self.fin, self.gs, KXY - 1, self.other).wait_recv()
+        self.c_copy(self.c).start()
+
+    def wait(self):
+        self.c_copy(1 - self.c).wait_recv()
+
+    def drain_sums(self):
+        self.core_copy().wait_send()
+        whole(self.xy, self.xys, KXY - 1, self.other).wait_send()
+
+    def drain(self):
+        whole(self.z, self.zs, NZ - 1, self.other).wait_send()
+        whole(self.fin, self.gs, KXY - 1, self.other).wait_send()
+        self.c_copy(self.c).wait_send()
 
 
 def kernel(scale, *refs):
@@ -525,59 +590,51 @@
 
     head_sums(s.feat, s.a_p)
     for j in range(PAIRS):
-        s.a_p[j, HD:, :] = jnp.broadcast_to(mass[:, 128 * j : 128 * j + 128], (8, 128))
+        s.a_p[j, HD:, :] = mass[:, 128 * j : 128 * j + 128]
 
     def reduce_pairs(part, buf_y, buf_z, sem_y, sem_z):
         def put_y(i):
             t = at_y(i)
-            return remote(part.at[t], buf_y.at[i], sem_y.at[0, i], sem_y.at[1, i], dev_y(t))
+            return remote(part.at[t], buf_y.at[i], sem_y.at[0], sem_y.at[1], dev_y(t))
 
         def put_z(i):
             return remote(
-                buf_z.at[z], buf_z.at[z], sem_z.at[0, i], sem_z.at[1, i], dev_z(at_z(i))
+                buf_z.at[z], buf_z.at[z], sem_z.at[0], sem_z.at[1], dev_z(at_z(i))
             )
-
-        def got_z(i):
-            f = from_z(i)
-            return remote(buf_z.at[f], buf_z.at[f], sem_z.at[0, i], sem_z.at[1, i], dev_z(f))
 
         def start():
             each(NY - 1, lambda i: put_y(i).start())
 
         def middle():
-            each(NY - 1, lambda i: put_y(i).wait_recv())
+            whole(buf_y, sem_y, NY - 1, other).wait_recv()
             buf_z[z] = part[y] + buf_y[0] + buf_y[1] + buf_y[2]
             each(NZ - 1, lambda i: put_z(i).start())
 
         def finish():
-            each(NZ - 1, lambda i: got_z(i).wait_recv())
+            whole(buf_z, sem_z, NZ - 1, other).wait_recv()
             total = buf_z[0]
             for i in range(1, NZ):
                 total = total + buf_z[i]
             return total
 
         def drain():
-            each(NY - 1, lambda i: put_y(i).wait_send())
-            each(NZ - 1, lambda i: put_z(i).wait_send())
+            whole(buf_y, sem_y, NY - 1, other).wait_send()
+            whole(buf_z, sem_z, NZ - 1, other).wait_send()
 
         return start, middle, finish, drain
 
     def gather_pairs(buf, sem):
         def put(i):
-            return remote(buf.at[y], buf.at[y], sem.at[0, i], sem.at[1, i], dev_y(at_y(i)))
-
-        def got(i):
-            f = from_y(i)
-            return remote(buf.at[f], buf.at[f], sem.at[0, i], sem.at[1, i], dev_y(f))
+            return remote(buf.at[y], buf.at[y], sem.at[0], sem.at[1], dev_y(at_y(i)))
 
         def start():
             each(NY - 1, lambda i: put(i).start())
 
         def wait():
-            each(NY - 1, lambda i: got(i).wait_recv())
+            whole(buf, sem, NY - 1, other).wait_recv()
 
         def drain():
-            each(NY - 1, lambda i: put(i).wait_send())
+            whole(buf, sem, NY - 1, other).wait_send()
 
         return start, wait, drain
 
@@ -670,8 +727,7 @@
         if p == 0:
             e.v[:, 16:24, :] = tdot(s.spread[...], s.grh[...]).reshape(32, 8, C)
         e.core_start()
-    for e in early:
-        e.st1_start()
+    early[0].st1_start()
     b_middle()
 
     for r in range(0, ROWS, CH):
@@ -682,51 +738,7 @@
                 s.bdm[128 * g : 128 * g + 128, 256 * g : 256 * g + 256],
             )
 
-    def scatter_xy(src, buf, sem):
-        def put(i):
-            xx, yy = at_xy(i)
-            return remote(
-                src.at[xx * NY + yy], buf.at[i], sem.at[0, i], sem.at[1, i], dev_xy(xx, yy)
-            )
-
-        def start():
-            each(KXY - 1, lambda i: put(i).start())
-
-        def wait():
-            each(KXY - 1, lambda i: put(i).wait_recv())
-
-        def drain():
-            each(KXY - 1, lambda i: put(i).wait_send())
-
-        return start, wait, drain
-
-    def gather_xy(buf, sem):
-        def put(i):
-            return remote(
-                buf.at[own], buf.at[own], sem.at[0, i], sem.at[1, i], dev_xy(*at_xy(i))
-            )
-
-        def got(i):
-            xx, yy = from_xy(i)
-            f = c * KXY + xx * NY + yy
-            return remote(buf.at[f], buf.at[f], sem.at[0, i], sem.at[1, i], dev_xy(xx, yy))
-
-        def start():
-            each(KXY - 1, lambda i: put(i).start())
-
-        def wait():
-            each(KXY - 1, lambda i: got(i).wait_recv())
-
-        def drain():
-            each(KXY - 1, lambda i: put(i).wait_send())
-
-        return start, wait, drain
-
-    def gather_core(buf, sem):
-        mine, theirs = pl.ds(c * KXY, KXY), pl.ds((1 - c) * KXY, KXY)
-        put = remote(buf.at[mine], buf.at[mine], sem.at[0], sem.at[1], other)
-        got = remote(buf.at[theirs], buf.at[theirs], sem.at[0], sem.at[1], other)
-        return put.start, got.wait_recv, put.wait_send
+    early[1].st1_start()
 
     gm = b_finish()
     dv = hdot(gm, att, (1, 0))
@@ -739,7 +751,7 @@
     dtok = hdot(wt, dqkv, (1, 0))
     gsum = dtok * inv_mass
     s.b_m[y, 0:HD, :] = gsum
-    s.b_m[y, HD:, :] = jnp.broadcast_to(-jnp.sum(gsum * tokens, axis=0, keepdims=True), (8, 128))
+    s.b_m[y, HD:, :] = -jnp.sum(gsum * tokens, axis=0, keepdims=True)
     bm_start()
     for e in early:
         e.st2_start()
@@ -748,45 +760,46 @@
         s.bdg[64 * j : 64 * j + 64, 128 * j : 128 * j + 128] = spread_diag(s.b_m[j, 0:HD, :])
     gmass = jnp.concatenate([s.b_m[j, HD : HD + 1, :] for j in range(PAIRS)], axis=1)
 
-    for r in range(0, ROWS, CH):
-        rows = slice(r, r + CH)
-        ga = s.ga[rows, :] + gmass
-        ga = ga + jnp.concatenate(
-            [
-                dot(
-                    s.feat[rows, 128 * g : 128 * g + 128],
-                    s.bdg[128 * g : 128 * g + 128, 256 * g : 256 * g + 256],
-                )
-                for g in range(2)
-            ],
-            axis=1,
-        )
-        a = s.asg[rows, :]
-        gl = (a * (ga - seg_sum(a * ga, s.ones[...])) * inv_sharp).astype(BF16)
-        s.gl[rows, :] = gl
-        s.gp[rows, :] = jnp.concatenate(
-            [
-                dot_t(
-                    gl[:, 256 * g : 256 * g + 256],
-                    s.bdw[128 * g : 128 * g + 128, 256 * g : 256 * g + 256],
-                )
-                for g in range(2)
-            ],
-            axis=1,
-        ).astype(BF16)
-        s.gf[rows, :] = jnp.concatenate(
-            [
-                dot_t(
-                    s.ah[rows, 256 * g : 256 * g + 256],
-                    s.bdg[128 * g : 128 * g + 128, 256 * g : 256 * g + 256],
-                )
-                for g in range(2)
-            ],
-            axis=1,
-        ).astype(BF16)
-
-    s.l_all[:, 0:8, :] = tdot(s.nh[...], s.gf[...]).reshape(32, 8, C)
-    s.l_all[:, 8:16, :] = tdot(s.nh[...], s.gp[...]).reshape(32, 8, C)
+    late = [Late(s, p, (x, c, z, y), scale) for p in range(len(LATE))]
+    first, second = late
+    early[0].z_start()
+    s.gf[...] = jnp.concatenate(
+        [
+            dot_t(
+                s.ah[:, 256 * g : 256 * g + 256],
+                s.bdg[128 * g : 128 * g + 128, 256 * g : 256 * g + 256],
+            )
+            for g in range(2)
+        ],
+        axis=1,
+    ).astype(BF16)
+    first.all[...] = tdot(s.nh[...], s.gf[...]).reshape(32, 8, C)
+    first.core_start()
+    ga = s.ga[...] + gmass
+    ga = ga + jnp.concatenate(
+        [
+            dot(
+                s.feat[:, 128 * g : 128 * g + 128],
+                s.bdg[128 * g : 128 * g + 128, 256 * g : 256 * g + 256],
+            )
+            for g in range(2)
+        ],
+        axis=1,
+    )
+    a = s.asg[...]
+    gl = (a * (ga - seg_sum(a * ga, s.ones[...])) * inv_sharp).astype(BF16)
+    s.gl[...] = gl
+    s.gp[...] = jnp.concatenate(
+        [
+            dot_t(
+                gl[:, 256 * g : 256 * g + 256],
+                s.bdw[128 * g : 128 * g + 128, 256 * g : 256 * g + 256],
+            )
+            for g in range(2)
+        ],
+        axis=1,
+    ).astype(BF16)
+    second.all[:, 0:8, :] = tdot(s.nh[...], s.gp[...]).reshape(32, 8, C)
     slices = jnp.zeros((HD, 128), F32)
     for g in range(2):
         t = tdot(s.proj[:, 128 * g : 128 * g + 128], s.gl[:, 256 * g : 256 * g + 256])
@@ -795,23 +808,11 @@
     tokenmap = jnp.where(z == 0, tokenmap, jnp.zeros_like(tokenmap))
     small = jnp.concatenate([slices, tokenmap, jnp.zeros((HD, 32), F32)], axis=1)
     for i in range(32):
-        s.l_all[i, 16:17, :] = small[i : i + 1, :]
-    l_core = remote(
-        s.l_all.at[pl.ds((1 - c) * KXY, KXY)], s.l_core, s.l_cs.at[0], s.l_cs.at[1], other
-    )
-    l_core.start()
-
-    l_core.wait_recv()
-
-    def add_core_late(i):
-        s.l_core[i] = s.l_core[i] + s.l_all[c * KXY + i]
-
-    each(KXY, add_core_late)
-    lx_start, lx_wait, lx_drain = scatter_xy(s.l_core, s.l_xy, s.l_xys)
-    lx_start()
-
-    for e in early:
-        e.z_start()
+        second.all[i, 8:9, :] = small[i : i + 1, :]
+    second.core_start()
+    first.xy_start()
+    second.xy_start()
+    early[1].z_start()
 
     for r in range(0, ROWS, CH):
         rows = slice(r, r + CH)
@@ -819,45 +820,39 @@
         gn = dot_t(s.gf[rows, :], s.wa[...]) + dot_t(s.gp[rows, :], s.wp[...])
         s.pgr[rows, :] = (s.gres[rows, :] + norm_back(normed, inv, gn)).astype(BF16)
     write(s.pgr, o_pg)
-
+    a_drain()
+    am_drain()
+    b_drain()
+    bm_drain()
     for e in early:
-        e.zg_start()
-
-    lx_wait()
-    part = s.l_core[k]
-    for i in range(KXY - 1):
-        part = part + s.l_xy[i]
-    s.l_z[z] = part
-
-    def l_putz(i):
-        return remote(
-            s.l_z.at[z], s.l_z.at[z], s.l_zs.at[0, i], s.l_zs.at[1, i], dev_z(at_z(i))
-        )
-
-    def l_gotz(i):
-        f = from_z(i)
-        return remote(s.l_z.at[f], s.l_z.at[f], s.l_zs.at[0, i], s.l_zs.at[1, i], dev_z(f))
-
-    each(NZ - 1, lambda i: l_putz(i).start())
-
-    for e in early:
-        e.st2g_start()
-    each(NZ - 1, lambda i: l_gotz(i).wait_recv())
-    total = s.l_z[0]
-    for i in range(1, NZ):
-        total = total + s.l_z[i]
-    s.l_fin[own] = total * scale
-    lg_start, lg_wait, lg_drain = gather_xy(s.l_fin, s.l_xygs)
-    lg_start()
-
-    for e in early:
-        e.st1g_start()
+        e.drain_sums()
+
+    early[0].zg_start()
+    first.z_start()
+    early[1].zg_start()
+    second.z_start()
+    early[0].st2g_start()
+    first.g_start()
+    early[1].st2g_start()
+    second.g_start()
+    early[0].st1g_start()
+    early[1].st1g_start()
+    for part in late:
+        part.drain_sums()
+    first.c_start()
+    second.c_start()
     early[0].coreg_start()
-    lg_wait()
-    lc_start, lc_wait, lc_drain = gather_core(s.l_fin, s.l_cgs)
-    lc_start()
-    for e in early[1:]:
-        e.coreg_start()
+    early[1].coreg_start()
+    for part in late:
+        part.wait()
+    write(first.fin, o_feat)
+    write(second.fin.at[:, pl.ds(0, 8), :], o_proj)
+    rows = [second.fin[i, 8:9, :] for i in range(32)]
+    small = jnp.concatenate(rows, axis=0)
+    s.slc[...] = small[:, 0:SL] + small[:, SL : 2 * SL]
+    s.tok[...] = small[:, 128 : 128 + 3 * HD]
+    write(s.slc, o_slice)
+    write(s.tok, o_tok)
     for p, e in enumerate(early):
         e.coreg_wait()
         for b in range(2):
@@ -867,25 +862,8 @@
         write(e.vf.at[:, pl.ds(0, 16), :], o_down.at[pl.ds(32 * p, 32)])
         if p == 0:
             write(e.vf.at[:, pl.ds(16, 8), :], o_out)
-    lc_wait()
-    write(s.l_fin.at[:, pl.ds(0, 8), :], o_feat)
-    write(s.l_fin.at[:, pl.ds(8, 8), :], o_proj)
-    rows = [s.l_fin[i, 16:17, :] for i in range(32)]
-    small = jnp.concatenate(rows, axis=0)
-    s.slc[...] = small[:, 0:SL] + small[:, SL : 2 * SL]
-    s.tok[...] = small[:, 128 : 128 + 3 * HD]
-    write(s.slc, o_slice)
-    write(s.tok, o_tok)
-
-    a_drain()
-    am_drain()
-    b_drain()
-    bm_drain()
-    l_core.wait_send()
-    lx_drain()
-    each(NZ - 1, lambda i: l_putz(i).wait_send())
-    lg_drain()
-    lc_drain()
+    for part in late:
+        part.drain()
     for e in early:
         e.drain()
     for copy in outs:

time: 85.4 us -> 79 us (0.925)
  Pallas kernels: 84.6 us -> 78.3 us
    pallas_call x1, Pallas kernels: 81.3 us -> 74.9 us  [body(): pl.pallas_call(functools.partial(kernel, scale), out_shape=results, in_sp...]
where the time goes in v3:
time: 79 us; the launch traced here: 78.9 us
  Pallas kernels  78.3 us (99%)
    pallas_call x1, Pallas kernels, body(): pl.pallas_call(functools.partial(kernel, scale), out_shape=results, in_sp...  74.9 us
    pallas_call x1, Pallas kernels, body(): pl.pallas_call(store, out_shape=results, in_specs=[hbm] * 9, out_specs=(h...  3.33 us

profile of v3, /device:TPU:1, one launch (start us, length us, event | category | flops | bytes accessed | tf_op | source)
XLA Modules:
  0.0 78.9 jit_solution(11813165678211679602)
XLA Ops:
  0.6 74.9 %layer.1 = (bf16[512,256]{1,0:T(8,128)(2,1)}, bf16[512,256]{1,0:T(8,128)(2,1)}, f32[32,8,256]{2,1,0:T(8,128)}, f32[32,8,256]{2,1,0:T(8,128)}, f32[32,64]{1,0:T(8...) custom-call(bf16[512,256]{1,0:T(8,128)(2,1)} %bitcast.9, ...), custom_call_target="tpu_custom_call" | custom-call | tf_op jit(solution)/shard_map/layer/pallas_call | solution.py:900
  75.6 3.3 %store.1 = (bf16[512,256]{1,0:T(8,128)(2,1)}, bf16[512,256]{1,0:T(8,128)(2,1)}, f32[32,8,256]{2,1,0:T(8,128)}, f32[32,8,256]{2,1,0:T(8,128)}, f32[32,64]{1,0:T(8...) custom-call(bf16[512,256]{1,0:T(8,128)(2,1)} %get-tuple-element.27.refs_0_, ...), custom_call_target="tpu_custom_call" | custom-call | tf_op jit(solution)/shard_map/store/pallas_call | solution.py:911

commit v4 on v3

--- a/solution.py
+++ b/solution.py
@@ -20,7 +20,7 @@
 PAIRS = 4
 KXY = NX * NY
 PARTS = ((16, 24), (16, 16))
-LATE = (8, 9)
+LATE = (9,)
 CH = 512
 
 
@@ -114,6 +114,7 @@
     gf=pltpu.VMEM((ROWS, C), BF16),
     gp=pltpu.VMEM((ROWS, C), BF16),
     upd=pltpu.VMEM((ROWS, C), BF16),
+    res=pltpu.VMEM((ROWS, C), BF16),
     pgr=pltpu.VMEM((ROWS, C), BF16),
     slc=pltpu.VMEM((HD, SL), F32),
     tok=pltpu.VMEM((HD, 3 * HD), F32),
@@ -148,6 +149,26 @@
         zs=d(), zos=d(), zgs=d(), uygs=d(), vxgs=d(), uxgs=d(3), vygs=d(3), ugs=d(4), vgs=d(4),
     )
     return {"e%d_%s" % (p, n): spec for n, spec in names.items()}
+
+
+SCRATCH.update(
+    n_all=pltpu.VMEM((PAIRS, C, 128), F32),
+    n_y=pltpu.VMEM((3, C, 128), F32),
+    n_sum=pltpu.VMEM((C, 128), F32),
+    n_z=pltpu.VMEM((NZ, 32, 128), F32),
+    f_own=pltpu.VMEM((16, 128), F32),
+    f_core=pltpu.VMEM((16, 128), F32),
+    f_x=pltpu.VMEM((NX, 16, 128), F32),
+    f_all=pltpu.VMEM((NC, NY, NZ, 8, 128), F32),
+    f_out=pltpu.VMEM((NZ, 4, 8, C), F32),
+    n_ys=pltpu.SemaphoreType.DMA((2,)),
+    n_zs=pltpu.SemaphoreType.DMA((2,)),
+    f_cs=pltpu.SemaphoreType.DMA((2,)),
+    f_xs=pltpu.SemaphoreType.DMA((2,)),
+    f_zs=pltpu.SemaphoreType.DMA((2,)),
+    f_ys=pltpu.SemaphoreType.DMA((2,)),
+    f_gs=pltpu.SemaphoreType.DMA((2,)),
+)
 
 
 def late_scratch(p, r):
@@ -643,6 +664,22 @@
     am_start, am_wait, am_drain = gather_pairs(s.a_m, s.a_ms)
     a_start()
     a_middle()
+
+    for g in range(2):
+        t = tdot(s.nh[...], s.ah[:, 256 * g : 256 * g + 256])
+        for j in range(2):
+            s.n_all[2 * g + j] = t[:, 128 * j : 128 * j + 128]
+
+    def n_puty(i):
+        t = at_y(i)
+        return remote(s.n_all.at[t], s.n_y.at[i], s.n_ys.at[0], s.n_ys.at[1], dev_y(t))
+
+    def n_putz(i):
+        t = at_z(i)
+        rows = pl.ds(pl.multiple_of(32 * t, 32), 32)
+        return remote(s.n_sum.at[rows], s.n_z.at[z], s.n_zs.at[0], s.n_zs.at[1], dev_z(t))
+
+    each(NY - 1, lambda i: n_puty(i).start())
     for i in (5, 1, 6, 7, 8):
         loads[i].wait()
     total = a_finish()
@@ -662,6 +699,11 @@
     am_wait()
     for j in range(PAIRS):
         s.bdm[64 * j : 64 * j + 64, 128 * j : 128 * j + 128] = spread_diag(s.a_m[j])
+
+    whole(s.n_y, s.n_ys, NY - 1, other).wait_recv()
+    s.n_sum[...] = s.n_all[y] + s.n_y[0] + s.n_y[1] + s.n_y[2]
+    each(NZ - 1, lambda i: n_putz(i).start())
+    s.n_z[z] = s.n_sum[pl.ds(pl.multiple_of(32 * z, 32), 32), :]
 
     for r in range(0, ROWS, CH):
         rows = slice(r, r + CH)
@@ -681,7 +723,7 @@
         n2h = n2.astype(BF16)
         s.n2h[rows, :] = n2h
         sens = s.ls[rows, :]
-        upd = res
+        s.res[rows, :] = res.astype(BF16)
         gn2 = jnp.zeros((CH, C), F32)
         for f in range(0, FF, 256):
             hid = dot(n2h, s.we[:, f : f + 256])
@@ -694,9 +736,7 @@
             gh = (gact * slope).astype(BF16)
             s.act[rows, f : f + 256] = acth
             s.gh[rows, f : f + 256] = gh
-            upd = upd + dot(acth, s.wd[f : f + 256, :])
             gn2 = gn2 + dot_t(gh, s.we[:, f : f + 256])
-        s.upd[rows, :] = upd.astype(BF16)
         gres = sens.astype(F32) + norm_back(n2, inv2, gn2)
         s.gres[rows, :] = gres
         grh = gres.astype(BF16)
@@ -714,7 +754,6 @@
         copy.start()
         outs.append(copy)
 
-    write(s.upd, o_upd)
 
     early = [Early(s, p, PARTS[p], (x, c, z, y), scale) for p in range(len(PARTS))]
     for p, e in enumerate(early):
@@ -739,6 +778,8 @@
             )
 
     early[1].st1_start()
+    s.upd[...] = (s.res[...].astype(F32) + dot(s.act[...], s.wd[...])).astype(BF16)
+    write(s.upd, o_upd)
 
     gm = b_finish()
     dv = hdot(gm, att, (1, 0))
@@ -753,28 +794,89 @@
     s.b_m[y, 0:HD, :] = gsum
     s.b_m[y, HD:, :] = -jnp.sum(gsum * tokens, axis=0, keepdims=True)
     bm_start()
+
+    whole(s.n_z, s.n_zs, NZ - 1, other).wait_recv()
+    nsum = s.n_z[0]
+    for i in range(1, NZ):
+        nsum = nsum + s.n_z[i]
+    nhi = nsum.astype(BF16)
+    nlo = (nsum - nhi.astype(F32)).astype(BF16)
+    gsd = spread_diag(gsum)
+    fblock = dot_t(nhi, gsd) + dot_t(nlo, gsd)
+    s.f_own[...] = jnp.concatenate([fblock[:16], fblock[16:]], axis=1)
+    f_core = remote(s.f_own, s.f_core, s.f_cs.at[0], s.f_cs.at[1], other)
+    f_core.start()
+
+    def f_putx(i):
+        t = lax.rem(x + i + 1, NX)
+        piece = s.f_x.at[x]
+        return remote(piece, piece, s.f_xs.at[0], s.f_xs.at[1], (t * NC + c, pt))
+
+    def f_x_start():
+        f_core.wait_recv()
+        s.f_x[x] = s.f_own[...] + s.f_core[...]
+        each(NX - 1, lambda i: f_putx(i).start())
+
+    def f_putz(i):
+        piece = s.f_all.at[c, y, z]
+        return remote(piece, piece, s.f_zs.at[0], s.f_zs.at[1], dev_z(at_z(i)))
+
+    def f_z_start():
+        whole(s.f_x, s.f_xs, NX - 1, other).wait_recv()
+        half = pl.ds(pl.multiple_of(8 * c, 8), 8)
+        total = s.f_x[0, half, :] + s.f_x[1, half, :] + s.f_x[2, half, :] + s.f_x[3, half, :]
+        s.f_all[c, y, z] = total * scale
+        each(NZ - 1, lambda i: f_putz(i).start())
+
+    def f_puty(i):
+        piece = s.f_all.at[c, y]
+        return remote(piece, piece, s.f_ys.at[0], s.f_ys.at[1], dev_y(at_y(i)))
+
+    def f_y_start():
+        whole(s.f_all.at[0, 0], s.f_zs, NZ - 1, other).wait_recv()
+        each(NY - 1, lambda i: f_puty(i).start())
+
+    def f_give(core):
+        piece = s.f_all.at[core]
+        return remote(piece, piece, s.f_gs.at[0], s.f_gs.at[1], other)
+
+    def f_give_start():
+        whole(s.f_all.at[0], s.f_ys, NY - 1, other).wait_recv()
+        f_give(c).start()
+
+    def f_finish():
+        f_give(1 - c).wait_recv()
+        left = lax.broadcasted_iota(jnp.int32, (64, 128), 1) < 64
+        for core in range(NC):
+            for j in range(2):
+                a0 = s.f_all[core, 2 * j].reshape(64, 128)
+                a1 = s.f_all[core, 2 * j + 1].reshape(64, 128)
+                lo = jnp.where(left, a0, pltpu.roll(a1, 64, 1))
+                hi = jnp.where(left, pltpu.roll(a0, 64, 1), a1)
+                lanes = slice(128 * j, 128 * j + 128)
+                s.f_out[:, core, :, lanes] = lo.reshape(NZ, 8, 128)
+                s.f_out[:, 2 + core, :, lanes] = hi.reshape(NZ, 8, 128)
+
+    def f_drain():
+        whole(s.n_y, s.n_ys, NY - 1, other).wait_send()
+        whole(s.n_z, s.n_zs, NZ - 1, other).wait_send()
+        f_core.wait_send()
+        whole(s.f_x, s.f_xs, NX - 1, other).wait_send()
+        whole(s.f_all.at[0, 0], s.f_zs, NZ - 1, other).wait_send()
+        whole(s.f_all.at[0], s.f_ys, NY - 1, other).wait_send()
+        f_give(c).wait_send()
+
     for e in early:
         e.st2_start()
+    f_x_start()
     bm_wait()
     for j in range(PAIRS):
         s.bdg[64 * j : 64 * j + 64, 128 * j : 128 * j + 128] = spread_diag(s.b_m[j, 0:HD, :])
     gmass = jnp.concatenate([s.b_m[j, HD : HD + 1, :] for j in range(PAIRS)], axis=1)
 
     late = [Late(s, p, (x, c, z, y), scale) for p in range(len(LATE))]
-    first, second = late
+    second = late[0]
     early[0].z_start()
-    s.gf[...] = jnp.concatenate(
-        [
-            dot_t(
-                s.ah[:, 256 * g : 256 * g + 256],
-                s.bdg[128 * g : 128 * g + 128, 256 * g : 256 * g + 256],
-            )
-            for g in range(2)
-        ],
-        axis=1,
-    ).astype(BF16)
-    first.all[...] = tdot(s.nh[...], s.gf[...]).reshape(32, 8, C)
-    first.core_start()
     ga = s.ga[...] + gmass
     ga = ga + jnp.concatenate(
         [
@@ -810,9 +912,19 @@
     for i in range(32):
         second.all[i, 8:9, :] = small[i : i + 1, :]
     second.core_start()
-    first.xy_start()
+    f_z_start()
     second.xy_start()
     early[1].z_start()
+    s.gf[...] = jnp.concatenate(
+        [
+            dot_t(
+                s.ah[:, 256 * g : 256 * g + 256],
+                s.bdg[128 * g : 128 * g + 128, 256 * g : 256 * g + 256],
+            )
+            for g in range(2)
+        ],
+        axis=1,
+    ).astype(BF16)
 
     for r in range(0, ROWS, CH):
         rows = slice(r, r + CH)
@@ -828,24 +940,25 @@
         e.drain_sums()
 
     early[0].zg_start()
-    first.z_start()
+    f_y_start()
     early[1].zg_start()
     second.z_start()
     early[0].st2g_start()
-    first.g_start()
+    f_give_start()
     early[1].st2g_start()
     second.g_start()
     early[0].st1g_start()
     early[1].st1g_start()
+    f_finish()
+    write(s.f_out, o_feat)
+    f_drain()
     for part in late:
         part.drain_sums()
-    first.c_start()
     second.c_start()
     early[0].coreg_start()
     early[1].coreg_start()
     for part in late:
         part.wait()
-    write(first.fin, o_feat)
     write(second.fin.at[:, pl.ds(0, 8), :], o_proj)
     rows = [second.fin[i, 8:9, :] for i in range(32)]
     small = jnp.concatenate(rows, axis=0)
@@ -872,13 +985,19 @@
 
 def store(*refs):
     held, outs, stage, sem = refs[:9], refs[9:18], refs[18:27], refs[27]
-    loads = [pltpu.make_async_copy(held[i], stage[i], sem.at[0, i]) for i in range(9)]
-    stores = [pltpu.make_async_copy(stage[i], outs[i], sem.at[1, i]) for i in range(9)]
+    parts = [(7, pl.ds(8 * q, 8)) for q in range(4)]
+    parts += [(8, pl.ds(16 * q, 16)) for q in range(4)]
+    parts += [(i, pl.ds(0, held[i].shape[0])) for i in (0, 1, 2, 3, 6, 4, 5)]
+    loads, stores = [], []
+    for n, (i, rows) in enumerate(parts):
+        piece = stage[i].at[rows]
+        loads.append(pltpu.make_async_copy(held[i].at[rows], piece, sem.at[0, n]))
+        stores.append(pltpu.make_async_copy(piece, outs[i].at[rows], sem.at[1, n]))
     for copy in loads:
         copy.start()
-    for i in range(9):
-        loads[i].wait()
-        stores[i].start()
+    for n in range(len(parts)):
+        loads[n].wait()
+        stores[n].start()
     for copy in stores:
         copy.wait()
 
@@ -889,7 +1008,7 @@
     results = (
         jax.ShapeDtypeStruct((ROWS, C), BF16),
         jax.ShapeDtypeStruct((ROWS, C), BF16),
-        jax.ShapeDtypeStruct((32, 8, C), F32),
+        jax.ShapeDtypeStruct((NZ, 4, 8, C), F32),
         jax.ShapeDtypeStruct((32, 8, C), F32),
         jax.ShapeDtypeStruct((HD, SL), F32),
         jax.ShapeDtypeStruct((HD, 3 * HD), F32),
@@ -914,7 +1033,7 @@
         in_specs=[hbm] * 9,
         out_specs=(hbm,) * 9,
         scratch_shapes=[pltpu.VMEM(r.shape, r.dtype) for r in results]
-        + [pltpu.SemaphoreType.DMA((2, 9))],
+        + [pltpu.SemaphoreType.DMA((2, 15))],
         compiler_params=pltpu.CompilerParams(vmem_limit_bytes=58 << 20),
         name="store",
     )(*held)

time: 79 us -> 77.8 us (0.985)
  Pallas kernels: 78.3 us -> 77 us
    pallas_call x1, Pallas kernels: 74.9 us -> 74 us  [body(): pl.pallas_call(functools.partial(kernel, scale), out_shape=results, in_sp...]
where the time goes in v4:
time: 77.8 us; the launch traced here: 77.6 us
  Pallas kernels  77 us (99%)
    pallas_call x1, Pallas kernels, body(): pl.pallas_call(functools.partial(kernel, scale), out_shape=results, in_sp...  74 us
    pallas_call x1, Pallas kernels, body(): pl.pallas_call(store, out_shape=results, in_specs=[hbm] * 9, out_specs=(h...  3.02 us

profile of v4, /device:TPU:1, one launch (start us, length us, event | category | flops | bytes accessed | tf_op | source)
XLA Modules:
  0.0 77.6 jit_solution(4873822282473013065)
XLA Ops:
  0.6 74.0 %layer.1 = (bf16[512,256]{1,0:T(8,128)(2,1)}, bf16[512,256]{1,0:T(8,128)(2,1)}, f32[8,4,8,256]{3,2,1,0:T(8,128)}, f32[32,8,256]{2,1,0:T(8,128)}, f32[32,64]{1,0:...) custom-call(bf16[512,256]{1,0:T(8,128)(2,1)} %bitcast.9, ...), custom_call_target="tpu_custom_call" | custom-call | tf_op jit(solution)/shard_map/layer/pallas_call | solution.py:1019
  74.6 3.0 %store.1 = (bf16[512,256]{1,0:T(8,128)(2,1)}, bf16[512,256]{1,0:T(8,128)(2,1)}, f32[8,4,8,256]{3,2,1,0:T(8,128)}, f32[32,8,256]{2,1,0:T(8,128)}, f32[32,64]{1,0:...) custom-call(bf16[512,256]{1,0:T(8,128)(2,1)} %get-tuple-element.27.refs_0_, ...), custom_call_target="tpu_custom_call" | custom-call | tf_op jit(solution)/shard_map/store/pallas_call | solution.py:1030

commit v5 on v4

--- a/solution.py
+++ b/solution.py
@@ -526,6 +526,11 @@
     def dev_xy(xx, yy):
         return (xx * NC + c, z * NY + yy)
 
+    in_dst = (s.mp, s.ls, s.wa, s.wp, s.ws, s.wt, s.wc, s.we, s.wd)
+    loads = [pltpu.make_async_copy(a, b, s.in_sem.at[i]) for i, (a, b) in enumerate(zip(ins, in_dst))]
+    order = (0, 2, 3, 4, 5, 1, 6, 7, 8)
+    for i in order:
+        loads[i].start()
     barrier = pltpu.get_barrier_semaphore()
     pl.semaphore_signal(barrier, inc=1, device_id=other, device_id_type=MESH)
     each(
@@ -539,11 +544,6 @@
         lambda i: pl.semaphore_signal(barrier, inc=1, device_id=dev_z(at_z(i)), device_id_type=MESH),
     )
 
-    in_dst = (s.mp, s.ls, s.wa, s.wp, s.ws, s.wt, s.wc, s.we, s.wd)
-    loads = [pltpu.make_async_copy(a, b, s.in_sem.at[i]) for i, (a, b) in enumerate(zip(ins, in_dst))]
-    order = (0, 2, 3, 4, 5, 1, 6, 7, 8)
-    for i in order:
-        loads[i].start()
     sharp_ref = ins[9]
 
     lane = lax.broadcasted_iota(jnp.int32, (1, 512), 1)
@@ -781,6 +781,7 @@
     s.upd[...] = (s.res[...].astype(F32) + dot(s.act[...], s.wd[...])).astype(BF16)
     write(s.upd, o_upd)
 
+    early[0].st2_start()
     gm = b_finish()
     dv = hdot(gm, att, (1, 0))
     datt = hdot(gm, v, (0, 0))
@@ -866,8 +867,6 @@
         whole(s.f_all.at[0], s.f_ys, NY - 1, other).wait_send()
         f_give(c).wait_send()
 
-    for e in early:
-        e.st2_start()
     f_x_start()
     bm_wait()
     for j in range(PAIRS):
@@ -912,6 +911,7 @@
     for i in range(32):
         second.all[i, 8:9, :] = small[i : i + 1, :]
     second.core_start()
+    early[1].st2_start()
     f_z_start()
     second.xy_start()
     early[1].z_start()
@@ -940,22 +940,22 @@
         e.drain_sums()
 
     early[0].zg_start()
+    early[1].zg_start()
     f_y_start()
-    early[1].zg_start()
+    early[0].st2g_start()
     second.z_start()
-    early[0].st2g_start()
+    early[1].st2g_start()
+    early[0].st1g_start()
     f_give_start()
-    early[1].st2g_start()
     second.g_start()
-    early[0].st1g_start()
     early[1].st1g_start()
     f_finish()
     write(s.f_out, o_feat)
     f_drain()
     for part in late:
         part.drain_sums()
+    early[0].coreg_start()
     second.c_start()
-    early[0].coreg_start()
     early[1].coreg_start()
     for part in late:
         part.wait()

time: 77.8 us -> 75.9 us (0.976)
  Pallas kernels: 77 us -> 75.1 us
    pallas_call x1, Pallas kernels: 74 us -> 72.1 us  [body(): pl.pallas_call(functools.partial(kernel, scale), out_shape=results, in_sp...]
where the time goes in v5:
time: 75.9 us; the launch traced here: 75.7 us
  Pallas kernels  75.1 us (99%)
    pallas_call x1, Pallas kernels, body(): pl.pallas_call(functools.partial(kernel, scale), out_shape=results, in_sp...  72.1 us
    pallas_call x1, Pallas kernels, body(): pl.pallas_call(store, out_shape=results, in_specs=[hbm] * 9, out_specs=(h...  3.02 us

profile of v5, /device:TPU:1, one launch (start us, length us, event | category | flops | bytes accessed | tf_op | source)
XLA Modules:
  0.0 75.7 jit_solution(6697208347752888216)
XLA Ops:
  0.6 72.1 %layer.1 = (bf16[512,256]{1,0:T(8,128)(2,1)}, bf16[512,256]{1,0:T(8,128)(2,1)}, f32[8,4,8,256]{3,2,1,0:T(8,128)}, f32[32,8,256]{2,1,0:T(8,128)}, f32[32,64]{1,0:...) custom-call(bf16[512,256]{1,0:T(8,128)(2,1)} %bitcast.9, ...), custom_call_target="tpu_custom_call" | custom-call | tf_op jit(solution)/shard_map/layer/pallas_call | solution.py:1019
  72.7 3.0 %store.1 = (bf16[512,256]{1,0:T(8,128)(2,1)}, bf16[512,256]{1,0:T(8,128)(2,1)}, f32[8,4,8,256]{3,2,1,0:T(8,128)}, f32[32,8,256]{2,1,0:T(8,128)}, f32[32,64]{1,0:...) custom-call(bf16[512,256]{1,0:T(8,128)(2,1)} %get-tuple-element.27.refs_0_, ...), custom_call_target="tpu_custom_call" | custom-call | tf_op jit(solution)/shard_map/store/pallas_call | solution.py:1030

commit v6 on v5

--- a/solution.py
+++ b/solution.py
@@ -912,9 +912,9 @@
         second.all[i, 8:9, :] = small[i : i + 1, :]
     second.core_start()
     early[1].st2_start()
-    f_z_start()
     second.xy_start()
     early[1].z_start()
+    f_z_start()
     s.gf[...] = jnp.concatenate(
         [
             dot_t(

time: 75.9 us -> 76.4 us (level)
  no operation moved by 1% of the time
where the time goes in v6:
time: 76.4 us; the launch traced here: 76.3 us
  Pallas kernels  75.7 us (99%)
    pallas_call x1, Pallas kernels, body(): pl.pallas_call(functools.partial(kernel, scale), out_shape=results, in_sp...  72.6 us
    pallas_call x1, Pallas kernels, body(): pl.pallas_call(store, out_shape=results, in_specs=[hbm] * 9, out_specs=(h...  3.02 us

profile of v6, /device:TPU:1, one launch (start us, length us, event | category | flops | bytes accessed | tf_op | source)
XLA Modules:
  0.0 76.3 jit_solution(8243945733271478448)
XLA Ops:
  0.6 72.6 %layer.1 = (bf16[512,256]{1,0:T(8,128)(2,1)}, bf16[512,256]{1,0:T(8,128)(2,1)}, f32[8,4,8,256]{3,2,1,0:T(8,128)}, f32[32,8,256]{2,1,0:T(8,128)}, f32[32,64]{1,0:...) custom-call(bf16[512,256]{1,0:T(8,128)(2,1)} %bitcast.9, ...), custom_call_target="tpu_custom_call" | custom-call | tf_op jit(solution)/shard_map/layer/pallas_call | solution.py:1019
  73.3 3.0 %store.1 = (bf16[512,256]{1,0:T(8,128)(2,1)}, bf16[512,256]{1,0:T(8,128)(2,1)}, f32[8,4,8,256]{3,2,1,0:T(8,128)}, f32[32,8,256]{2,1,0:T(8,128)}, f32[32,64]{1,0:...) custom-call(bf16[512,256]{1,0:T(8,128)(2,1)} %get-tuple-element.27.refs_0_, ...), custom_call_target="tpu_custom_call" | custom-call | tf_op jit(solution)/shard_map/store/pallas_call | solution.py:1030
